TPU v7x, 128 devices: a whole 4x4x4 slice. The times are simulated.
128 devices in a mesh: lon: 8 (over x, y_hi), lat: 16 (over z, y_lo, core).
Axes of the slice: x: 4, y: 4 (y_hi: 2, y_lo: 2; y = y_hi * 2 + y_lo), z: 4, core: 2. Of those that a mesh axis runs over, the one named last changes fastest.
Arguments:
- atmos: float32 [4, 16, 1024, 2048], P(None, None, 'lat', 'lon'), may hold values from -6 to 6
- previous_surface_heat: float32 [1024, 2048], P('lat', 'lon'), may hold values from -4 to 4
- insolation: float32 [1024, 2048], P('lat', 'lon'), may hold values from 0 to 2
- regrid_weight: bfloat16 [16384, 3, 128, 128], P(('lon', 'lat')), may hold values from -0.3125 to 0.3125
- destination_device: int32 [16384, 3], P(('lon', 'lat')), may hold values from 0 to 127, as said below
- destination_tile: int32 [16384, 3], P(('lon', 'lat')), may hold values from 0 to 95
- atmosphere_mixer: float32 [16, 16], replicated, may hold values from -1.5 to 1.5
- ocean: float32 [4, 16, 768, 2048], P(None, None, 'lat', 'lon'), may hold values from -6 to 6
- water_mask: int32 [768, 2048], P('lat', 'lon'), may hold values 0 or 1
- seam_column_index: int32 [2048], P('lon'), may hold values from 0 to 2047, as said below
- marine_mixer: float32 [16, 16], replicated, may hold values from -1.5 to 1.5
Outputs:
- atmosphere_final: float32 [4, 16, 1024, 2048], P(None, None, 'lat', 'lon')
- exchanged_surface_heat: float32 [1024, 2048], P('lat', 'lon')
- marine_final: float32 [4, 16, 768, 2048], P(None, None, 'lat', 'lon')
- marine_surface_flux: float32 [8, 768, 2048], P(None, 'lat', 'lon')
Inputs may be any that keep to these rules, and one draw needn't show every extreme that they name: `destination_device`: each row names 3 different owners; each owner's lon index is within one of the lon index of the tile's own block (cyclically over 8) and its lat index within one of the block's lat index. seam_column_index[c] = (p - c) mod 2048 for one p of the draw, so the map is its own inverse.
All inputs are finite; a program needn't handle non-finite values. No bound on the sum of `water_mask` on one device may be relied on, other than what follows from the above.
Results may differ from a plain program's by a relative error of at most 0.003.
Values may be sent and summed in bfloat16 or wider, within the bound.
A program may use at most 192 MiB of HBM per device.

v0:
```python
import functools

import jax
import jax.numpy as jnp
from jax import lax
from jax.experimental import pallas as pl
from jax.experimental.pallas import tpu as pltpu
from jax.sharding import PartitionSpec as P

F32 = jnp.float32
BF = jnp.bfloat16
MESH = pl.DeviceIdType.MESH
HIGHEST = lax.Precision.HIGHEST
NT = (((1,), (1,)), ((), ()))
TN = (((0,), (0,)), ((), ()))
N_LON = 8
N_LAT = 16
STEPS = 4
MIB = 2**20


def flux_fields(u, v, ta, qa, ts, sw):
    speed = jnp.sqrt(u * u + v * v + 1.0)
    soft = jnp.maximum(qa, 0.0) + jnp.log1p(jnp.exp(-jnp.abs(qa)))
    return [
        0.8 * speed * u,
        0.8 * speed * v,
        0.6 * speed * (ts - ta),
        0.5 * speed * (0.4 * jnp.exp(0.5 * ts) - qa),
        0.3 * (ta - ts) * (2.0 + jnp.tanh(ta)),
        sw * (0.9 - 0.1 * jnp.tanh(qa)),
        soft,
        0.3 * speed * speed,
    ]


def slot_rows(owner, tile):
    lon = lax.axis_index("lon")
    lat = lax.axis_index("lat")
    lon_offset = ((owner >> 4) - lon + 1) & 7
    lat_offset = (owner & 15) - lat + 1
    return (lon_offset * 3 + lat_offset) * 96 + tile


def one_hot_slots(dd, dt, k):
    slot = slot_rows(dd[k : k + 1, :], dt[k : k + 1, :])
    rows = lax.broadcasted_iota(jnp.int32, (864, 128), 0)
    return jnp.where(slot == rows, 1.0, 0.0).astype(BF)


def out_kernel(surf, ts, sw, dd, dt, atm, oce, mask, w, send, rows, cols, corn, ft, terms, oh, tb, rbuf, cbuf):
    i = pl.program_id(0)
    tiles = w.shape[0]
    fields = atm.shape[0]

    @pl.when(i == 0)
    def _():
        vals = flux_fields(surf[0, 0], surf[1, 0], surf[2, 0], surf[3, 0], ts[...], sw[...])
        for f, val in enumerate(vals):
            val = val.astype(BF).astype(F32)
            ft[pl.ds(f, 64, stride=16), :] = val[:, :128]
            ft[pl.ds(8 + f, 64, stride=16), :] = val[:, 128:]
        for k in range(3):
            oh[:, k * 128 : (k + 1) * 128] = one_hot_slots(dd, dt, k)
        cbuf[...] = jnp.zeros_like(cbuf)
        rbuf[...] = jnp.zeros_like(rbuf)

    group = lax.broadcasted_iota(jnp.int32, (32, 128), 0)
    even = (group & 8) == 0
    for j in range(0, tiles, 4):
        t = i * tiles + j
        a = ft[pl.ds(pl.multiple_of(t * 8, 32), 32), :]
        lhs = jnp.concatenate([jnp.where(even, a, 0.0), jnp.where(even, 0.0, a)], axis=1).astype(BF)
        for h in range(2):
            q = j + 2 * h
            block = jnp.concatenate(
                [jnp.concatenate([w[q, 0], w[q, 1]], axis=1), jnp.concatenate([w[q + 1, 0], w[q + 1, 1]], axis=1)], axis=0
            )
            r = jnp.dot(lhs[16 * h : 16 * h + 16], block, preferred_element_type=F32)
            for k in range(2):
                terms[pl.ds(pl.multiple_of((k * 128 + t + 2 * h) * 8, 16), 16), :] = r[:, k * 128 : (k + 1) * 128]
        block = jnp.concatenate(
            [jnp.concatenate([w[j, 2], w[j + 2, 2]], axis=1), jnp.concatenate([w[j + 1, 2], w[j + 3, 2]], axis=1)], axis=0
        )
        r = jnp.dot(lhs, block, preferred_element_type=F32)
        at = pl.multiple_of((256 + t) * 8, 32)
        terms[pl.ds(at, 16), :] = r[:16, :128]
        terms[pl.ds(at + 16, 16), :] = r[16:, 128:]

    lane_a = lax.broadcasted_iota(jnp.int32, (64, 128), 1) >> 1
    lane_o = lax.broadcasted_iota(jnp.int32, (48, 128), 1) >> 1
    left_a, right_a = cbuf[0, 0:64, :], cbuf[1, 0:64, :]
    left_o, right_o = cbuf[0, 64:112, :], cbuf[1, 64:112, :]
    for j in range(fields):
        n = i * fields + j
        back = (2 * n + 2) & 127
        left_a = jnp.where(lane_a == n, pltpu.roll(atm[j, :, 0:128], 2 * n, 1), left_a)
        right_a = jnp.where(lane_a == n, pltpu.roll(atm[j, :, 128:256], back, 1), right_a)
        left_o = jnp.where(lane_o == n, pltpu.roll(oce[j, :, 0:128], 2 * n, 1), left_o)
        right_o = jnp.where(lane_o == n, pltpu.roll(oce[j, :, 128:256], back, 1), right_o)
        for e in range(2):
            rbuf[e, pl.ds(n, 1), :] = atm[j, e : e + 1, :]
            rbuf[2 + e, pl.ds(n, 1), :] = atm[j, 62 + e : 63 + e, :]
            rbuf[e, pl.ds(64 + n, 1), :] = oce[j, e : e + 1, :]
            rbuf[2 + e, pl.ds(64 + n, 1), :] = oce[j, 46 + e : 47 + e, :]
    cbuf[0, 0:64, :], cbuf[1, 0:64, :] = left_a, right_a
    cbuf[0, 64:112, :], cbuf[1, 64:112, :] = left_o, right_o

    @pl.when(i == pl.num_programs(0) - 1)
    def _():
        sea = mask[...].astype(F32)
        cbuf[0, 112:160, :] = sea[:, 0:128]
        cbuf[1, 112:160, :] = sea[:, 128:256]
        for e in range(2):
            rbuf[e, 128:129, :] = sea[e : e + 1, :]
            rbuf[2 + e, 128:129, :] = sea[46 + e : 47 + e, :]
        rows[...] = rbuf[...].astype(BF)
        cols[...] = cbuf[...].astype(BF)
        for side in range(2):
            corn[2 * side, 0:16, :] = cbuf[side, 0:16, :].astype(BF)
            corn[2 * side, 16:32, :] = cbuf[side, 64:80, :].astype(BF)
            corn[2 * side + 1, 0:16, :] = cbuf[side, 48:64, :].astype(BF)
            corn[2 * side + 1, 16:32, :] = cbuf[side, 96:112, :].astype(BF)
        for f in range(8):
            tb[:, f * 128 : (f + 1) * 128] = terms[pl.ds(f, 384, stride=8), :].astype(BF)
        for g in range(4):
            res = jnp.dot(oh[...], tb[:, g * 256 : (g + 1) * 256], preferred_element_type=F32)
            for o in range(9):
                for b in range(2):
                    send[o, 2 * g + b] = res[o * 96 : (o + 1) * 96, b * 128 : (b + 1) * 128].astype(BF)


def remap_out(atm, oce, ts, sw, w, dd, dt, mask):
    tiles = 128 // STEPS
    fields = 64 // STEPS
    whole = lambda *shape: pl.BlockSpec(shape, lambda i: (0,) * len(shape))
    return pl.pallas_call(
        out_kernel,
        grid=(STEPS,),
        in_specs=[
            pl.BlockSpec((4, 1, 64, 256), lambda i: (0, 15, 0, 0)),
            whole(64, 256),
            whole(64, 256),
            whole(3, 128),
            whole(3, 128),
            pl.BlockSpec((fields, 64, 256), lambda i: (i, 0, 0)),
            pl.BlockSpec((fields, 48, 256), lambda i: (i, 0, 0)),
            whole(48, 256),
            pl.BlockSpec((tiles, 3, 128, 128), lambda i: (i, 0, 0, 0)),
        ],
        out_specs=[whole(9, 8, 96, 128), whole(4, 144, 256), whole(2, 160, 128), whole(4, 32, 128)],
        out_shape=[
            jax.ShapeDtypeStruct((9, 8, 96, 128), BF),
            jax.ShapeDtypeStruct((4, 144, 256), BF),
            jax.ShapeDtypeStruct((2, 160, 128), BF),
            jax.ShapeDtypeStruct((4, 32, 128), BF),
        ],
        scratch_shapes=[
            pltpu.VMEM((1024, 128), F32),
            pltpu.VMEM((3072, 128), F32),
            pltpu.VMEM((864, 384), BF),
            pltpu.VMEM((384, 1024), BF),
            pltpu.VMEM((4, 144, 256), F32),
            pltpu.VMEM((2, 160, 128), F32),
        ],
        compiler_params=pltpu.CompilerParams(vmem_limit_bytes=40 * MIB),
        name="remap_out",
    )(atm, ts, sw, dd, dt, atm.reshape(64, 64, 256), oce.reshape(64, 48, 256), mask, w)


def step(x, rate):
    rows, lanes = x.shape
    around = pltpu.roll(x, 1, 0) + pltpu.roll(x, rows - 1, 0) + pltpu.roll(x, 1, 1) + pltpu.roll(x, lanes - 1, 1)
    return (1.0 - 4.0 * rate) * x + rate * around


def unpacked(from_left, from_right, n):
    lane = lax.broadcasted_iota(jnp.int32, from_left.shape, 1)
    right = pltpu.roll(from_right, (128 - 2 * n) & 127, 1)
    left = pltpu.roll(from_left, 126 - 2 * n, 1)
    return jnp.where(lane < 2, right, jnp.where(lane >= 126, left, 0.0))


def two_rows(at, first, second):
    rows = lax.broadcasted_iota(jnp.int32, (8, first.shape[1]), 0)
    return jnp.where(rows == at, first, jnp.where(rows == at + 1, second, 0.0))


def framed(x, south, north, third):
    return jnp.concatenate([jnp.concatenate([south, x, north], axis=0), third], axis=1)


def spread(mixer, cells):
    size = 16 * cells
    pick = lambda dim: jnp.where(
        lax.broadcasted_iota(jnp.int32, (size, 16) if dim == 0 else (16, size), dim) // cells
        == lax.broadcasted_iota(jnp.int32, (size, 16) if dim == 0 else (16, size), 1 - dim),
        1.0,
        0.0,
    )
    dot = functools.partial(jnp.dot, precision=HIGHEST, preferred_element_type=F32)
    full = dot(dot(pick(0), mixer), pick(1))
    r = lax.broadcasted_iota(jnp.int32, (size, size), 0) % cells
    c = lax.broadcasted_iota(jnp.int32, (size, size), 1) % cells
    return jnp.where(r == c, full, 0.0)


def halves(x):
    high = x.astype(BF)
    return high, (x - high.astype(F32)).astype(BF)


def dot3(lhs_high, lhs_low, x):
    high, low = halves(x)
    dot = functools.partial(jnp.dot, preferred_element_type=F32)
    return dot(lhs_high, high) + dot(lhs_high, low) + dot(lhs_low, high)


def middle_kernel(
    send, rows, cols, corn, atm, oce, mask, seam, mix_a, mix_o,
    stepped, ss, q_out, f_out, sst_out, coef_out,
    xa, xo, lla, bc, own, pr, ro, rl, sl, rr, cc, kk, fr, rrf, cea, ceo, gfc, mext, fold, uv,
    ka, ko, fs, dr_s, dr_r, dc_s, dc_r, dk_r, fd, drf, ced, gd, sst_s, sst_r,
    lsem, ssem, rsem,
):
    lon = lax.axis_index("lon")
    lat = lax.axis_index("lat")
    side = lax.rem(lat, 2)
    partner = lat + 1 - 2 * side
    outer = lat - 1 + 2 * side
    has_outer = jnp.logical_and(outer >= 0, outer < N_LAT)
    has_south = lat > 0
    has_north = lat < N_LAT - 1
    top = lat == N_LAT - 1
    always = lat >= 0
    lon_at = lambda d: lax.rem(lon + d + N_LON, N_LON)

    def lat_ok(d):
        return always if d == 0 else (has_south if d < 0 else has_north)

    def send_to(cond, src, dst, n, m, dev_lon, dev_lat):
        copy = pltpu.make_async_remote_copy(
            src_ref=src, dst_ref=dst, send_sem=ssem.at[n], recv_sem=rsem.at[m],
            device_id=(dev_lon, dev_lat), device_id_type=MESH,
        )

        @pl.when(cond)
        def _():
            copy.start()

        def finish():
            @pl.when(cond)
            def _():
                copy.wait_send()

        pending.append(finish)

    def arrive(cond, dst, m):
        @pl.when(cond)
        def _():
            pltpu.make_async_remote_copy(
                src_ref=dst, dst_ref=dst, send_sem=ssem.at[0], recv_sem=rsem.at[m],
                device_id=(lon, partner), device_id_type=MESH,
            ).wait_recv()

    pending = []
    loads = [
        pltpu.make_async_copy(oce, xo, lsem.at[0]),
        pltpu.make_async_copy(atm, xa, lsem.at[1]),
    ] + [pltpu.make_async_copy(send.at[dl * 3 + 1], own.at[dl], lsem.at[2 + dl]) for dl in range(3)]
    for load in loads:
        load.start()

    barrier = pltpu.get_barrier_semaphore()
    around = [(dl, dn) for dl in (-1, 0, 1) for dn in (-1, 0, 1) if (dl, dn) != (0, 0)]
    for dl, dn in around:

        @pl.when(lat_ok(dn))
        def _(dl=dl, dn=dn):
            pl.semaphore_signal(barrier, inc=1, device_id=(lon_at(dl), lat + dn), device_id_type=MESH)

    @pl.when(top)
    def _():
        for d in range(2, N_LON - 1):
            pl.semaphore_signal(barrier, inc=1, device_id=(lon_at(d), lat), device_id_type=MESH)
        pl.semaphore_wait(barrier, 5 + 5)

    @pl.when(lat == 0)
    def _():
        pl.semaphore_wait(barrier, 5)

    @pl.when(jnp.logical_and(has_south, has_north))
    def _():
        pl.semaphore_wait(barrier, 8)

    direction = {pair: n for n, pair in enumerate(around)}

    def halo(first, rows_s, rows_r, cols_s, cols_r, corn_s, corn_r):
        for dl, dn in around:
            n = first + direction[(dl, dn)]
            back = first + direction[(-dl, -dn)]
            if dl == 0:
                src, dst = rows_s(max(dn, 0)), rows_r(max(-dn, 0))
            elif dn == 0:
                src, dst = cols_s(max(dl, 0)), cols_r(max(-dl, 0))
            else:
                src, dst = corn_s(max(dl, 0), max(dn, 0)), corn_r(max(-dl, 0), max(-dn, 0))
            send_to(lat_ok(dn), src, dst, n, back, lon_at(dl), lat + dn)

    def halo_arrive(first, rows_r, cols_r, corn_r):
        for dl, dn in around:
            n = first + direction[(dl, dn)]
            if dl == 0:
                dst = rows_r(max(dn, 0))
            elif dn == 0:
                dst = cols_r(max(dl, 0))
            else:
                dst = corn_r(max(dl, 0), max(dn, 0))
            arrive(lat_ok(dn), dst, n)

    def ring(first, src, landing):
        for d in range(1, N_LON):
            send_to(top, src, landing.at[lon], first + d, first + lon, lon_at(d), lat)

    def ring_arrive(first, landing):
        for d in range(1, N_LON):
            arrive(top, landing.at[lon_at(d)], first + lon_at(d))

    rows_r = lambda b: rr.at[b]
    cols_r = lambda a: cc.at[a]
    corn_r = lambda a, b: kk.at[2 * a + b]
    halo(0, lambda b: rows.at[pl.ds(2 * b, 2)], rows_r, lambda a: cols.at[a], cols_r, lambda a, b: corn.at[2 * a + b], corn_r)
    fold_src = rows.at[pl.ds(2, 2), pl.ds(64, 80)]
    ring(8, fold_src, fr)
    own_fold = pltpu.make_async_copy(fold_src, fr.at[lon], lsem.at[5])

    @pl.when(top)
    def _():
        own_fold.start()

    for dl in (0, 2, 1):
        send_to(always, send.at[dl * 3 + 2 - 2 * side], pr.at[dl], 16 + dl, 16 + dl, lon, partner)
    for dl in range(3):
        send_to(has_outer, send.at[dl * 3 + 2 * side], ro.at[dl], 19 + dl, 19 + dl, lon_at(dl - 1), outer)

    @pl.when(jnp.logical_not(has_outer))
    def _():
        ro[...] = jnp.zeros_like(ro)

    for b, cond in ((0, has_south), (1, has_north)):

        @pl.when(jnp.logical_not(cond))
        def _(b=b):
            rr[b] = jnp.zeros(rr.shape[1:], BF)
            dr_r[b] = jnp.zeros(dr_r.shape[1:], BF)
            for a in range(2):
                kk[2 * a + b] = jnp.zeros(kk.shape[1:], BF)
                dk_r[2 * a + b] = jnp.zeros(dk_r.shape[1:], BF)
            for dl in range(3):
                sst_r[dl * 3 + 2 * b] = jnp.zeros(sst_r.shape[1:], BF)

    for load in loads[2:]:
        load.wait()
    for dl in (0, 2, 1):
        arrive(always, pr.at[dl], 16 + dl)
    for n, dl in enumerate((0, 2)):

        @pl.loop(0, 8)
        def _(f, n=n, dl=dl):
            sl[n, f] = (own[dl, f].astype(F32) + pr[dl, f].astype(F32)).astype(BF)

        send_to(always, sl.at[n], rl.at[n], 22 + n, 22 + n, lon_at(dl - 1), lat)

    ma = mix_a[...]
    mo = mix_o[...]
    dot = functools.partial(jnp.dot, precision=HIGHEST, preferred_element_type=F32)
    ma2 = dot(ma, ma)
    mo2 = dot(mo, mo)
    ka[0], ka[1] = halves(spread(ma2, 16))
    ko[0, :, 0:128], ko[1, :, 0:128] = halves(spread(mo2, 8))
    ko[0, :, 128:256], ko[1, :, 128:256] = halves(spread(mo, 8))
    coef = jnp.broadcast_to(mo2[:, 0:1], (16, 128))
    coef_out[...] = coef

    @pl.when(top)
    def _():
        lane = lax.broadcasted_iota(jnp.int32, (1, 384), 1)
        column = lon * 256 + jnp.where(lane < 320, lane, lane - 384)
        pole = seam[0:1, 0:1] + lon * 256
        source = (pole - column) & 2047
        for j in range(8):
            fold[j * 256 : (j + 1) * 256, :] = jnp.where(
                lax.broadcasted_iota(jnp.int32, (256, 384), 0) + j * 256 == source, 1.0, 0.0
            ).astype(BF)

    loads[0].wait()
    loads[1].wait()
    uv[0] = xo[2, 0]
    uv[1] = xo[3, 0]

    halo_arrive(0, rows_r, cols_r, corn_r)
    for b in range(2):
        for e in range(2):
            rrf[b, e] = rr[b, e].astype(F32)
    for a in range(2):
        side_cols = cc[a].astype(F32)
        ks = kk[2 * a].astype(F32)
        kn = kk[2 * a + 1].astype(F32)
        cea[a, 0:8, :] = ks[8:16]
        cea[a, 8:72, :] = side_cols[0:64]
        cea[a, 72:80, :] = kn[0:8]
        ceo[a, 0:8, :] = ks[24:32]
        ceo[a, 8:56, :] = side_cols[64:112]
        ceo[a, 56:64, :] = kn[16:24]

    @pl.when(top)
    def _():
        own_fold.wait()
        ring_arrive(8, fr)
        total = jnp.zeros((160, 384), F32)
        for j in range(8):
            total += jnp.dot(fr[j].reshape(160, 256), fold[j * 256 : (j + 1) * 256, :], preferred_element_type=F32)
        n = lax.broadcasted_iota(jnp.int32, (80, 384), 0)
        sign = jnp.where(jnp.logical_and(n >= 32, n < 64), -1.0, 1.0)
        for e in range(2):
            ghost = total[80 * (1 - e) : 80 * (2 - e)] * sign
            gfc[e] = ghost[:, 256:384]
            rrf[1, e, 64:144, :] = ghost[:, 0:256]

    @pl.when(jnp.logical_not(top))
    def _():
        gfc[...] = jnp.zeros_like(gfc)

    lane_m = lax.broadcasted_iota(jnp.int32, (48, 128), 1)
    sea = mask[...].astype(F32)
    third = jnp.where(
        lane_m < 2, cc[1, 112:160, :].astype(F32), jnp.where(lane_m >= 126, cc[0, 112:160, :].astype(F32), 0.0)
    )
    none = jnp.zeros((8, 128), F32)
    mext[...] = framed(
        sea,
        two_rows(6, rrf[0, 0, 128:129, :], rrf[0, 1, 128:129, :]),
        two_rows(0, rrf[1, 0, 128:129, :], rrf[1, 1, 128:129, :]),
        jnp.concatenate([none, third, none], axis=0),
    )

    @pl.loop(0, 64)
    def _(n):
        v = n // 16
        l = lax.rem(n, 16)
        third = unpacked(ceo[0], ceo[1], n)
        north = jnp.where(top, two_rows(0, gfc[0, pl.ds(n, 1), :], gfc[1, pl.ds(n, 1), :]), third[56:64])
        x = framed(
            xo[v, l],
            two_rows(6, rrf[0, 0, pl.ds(64 + n, 1), :], rrf[0, 1, pl.ds(64 + n, 1), :]),
            two_rows(0, rrf[1, 0, pl.ds(64 + n, 1), :], rrf[1, 1, pl.ds(64 + n, 1), :]),
            jnp.concatenate([third[0:56], north], axis=0),
        )
        m = mext[...]
        b = step(m * step(x, 0.2), 0.2)
        c = step(x - m * x, 0.2)
        bc[v, l] = b[8:56, 0:256]
        bc[v, 16 + l] = c[8:56, 0:256]

    @pl.loop(0, 24)
    def _(n):
        v = n // 6
        at = pl.multiple_of(lax.rem(n, 6) * 8, 8)
        mixed = dot3(ko[0], ko[1], bc[v, :, pl.ds(at, 8), :].reshape(256, 256)).reshape(16, 8, 256)
        wet = mask[pl.ds(at, 8), :] > 0
        xo[v, :, pl.ds(at, 8), :] = jnp.where(wet[None], mixed, xo[v, :, pl.ds(at, 8), :])

    ocean_out = pltpu.make_async_copy(xo, ss, lsem.at[0])
    ocean_out.start()

    row_a = lax.broadcasted_iota(jnp.int32, (80, 1), 0)
    inside = jnp.where(
        jnp.logical_and(jnp.logical_or(row_a >= 8, has_south), jnp.logical_or(row_a < 72, has_north)), 1.0, 0.0
    )

    @pl.loop(0, 64)
    def _(n):
        x = framed(
            xa[n // 16, lax.rem(n, 16)],
            two_rows(6, rrf[0, 0, pl.ds(n, 1), :], rrf[0, 1, pl.ds(n, 1), :]),
            two_rows(0, rrf[1, 0, pl.ds(n, 1), :], rrf[1, 1, pl.ds(n, 1), :]),
            unpacked(cea[0], cea[1], n),
        )
        y = step(inside * step(x, 0.15), 0.15)
        lla[n // 16, lax.rem(n, 16)] = y[8:72, 0:256]

    @pl.loop(0, 16)
    def _(n):
        v = n // 4
        at = pl.multiple_of(lax.rem(n, 4) * 16, 16)
        mixed = dot3(ka[0], ka[1], lla[v, :, pl.ds(at, 16), :].reshape(256, 256))
        xa[v, :, pl.ds(at, 16), :] = mixed.reshape(16, 16, 256)

    atm_out = pltpu.make_async_copy(xa, stepped, lsem.at[1])
    atm_out.start()

    for dl in range(3):
        arrive(has_outer, ro.at[dl], 19 + dl)
    for n in range(2):
        arrive(always, rl.at[n], 22 + n)

    @pl.loop(0, 8)
    def _(f):
        parts = [own[1, f], pr[1, f], rl[0, f], rl[1, f], ro[0, f], ro[1, f], ro[2, f]]
        total = functools.reduce(lambda x, y: x + y, [p.astype(F32) for p in parts])
        fs[pl.ds(pl.multiple_of(f * 96, 8), 96), :] = total

    flux = []
    for f in range(8):
        value = sea * jnp.concatenate([fs[pl.ds(f * 96 + h, 48, stride=2), :] for h in range(2)], axis=1)
        f_out[f] = value
        flux.append(value)
    forcing = [
        0.2 * sea * (flux[5] - flux[2] - flux[3] - flux[4]),
        0.2 * sea * (flux[3] - flux[6]),
        sea * (0.3 * flux[0] - 0.1 * flux[7] * uv[0]),
        sea * (0.3 * flux[1] - 0.1 * flux[7] * uv[1]),
    ]

    left = jnp.zeros((48, 128), F32)
    right = jnp.zeros((48, 128), F32)
    edge = [[jnp.zeros((16, 256), F32) for _ in range(2)] for _ in range(2)]
    row_16 = lax.broadcasted_iota(jnp.int32, (16, 256), 0)
    for f, d in enumerate(forcing):
        left = jnp.where((lane_m >> 1) == f, pltpu.roll(d[:, 0:128], 2 * f, 1) if f else d[:, 0:128], left)
        right = jnp.where((lane_m >> 1) == f, pltpu.roll(d[:, 128:256], 2 * f + 2, 1), right)
        for b in range(2):
            for e in range(2):
                r = 46 * b + e
                edge[b][e] = jnp.where(row_16 == f, d[r : r + 1, :], edge[b][e])
    dc_s[0] = left.astype(BF)
    dc_s[1] = right.astype(BF)
    for b in range(2):
        for e in range(2):
            dr_s[b, 16 * e : 16 * e + 16, :] = edge[b][e].astype(BF)
    rows_r = lambda b: dr_r.at[b]
    cols_r = lambda a: dc_r.at[a]
    corn_r = lambda a, b: dk_r.at[2 * a + b]
    halo(24, lambda b: dr_s.at[b], rows_r, lambda a: dc_s.at[a], cols_r,
         lambda a, b: dc_s.at[a, pl.ds(32 * b, 16)], corn_r)
    ring(32, dr_s.at[1], fd)

    @pl.when(top)
    def _():
        fd[lon] = dr_s[1]

    halo_arrive(24, rows_r, cols_r, corn_r)
    for b in range(2):
        drf[b] = dr_r[b].astype(F32)
    for a in range(2):
        ced[a, 0:8, :] = dk_r[2 * a].astype(F32)[8:16]
        ced[a, 8:56, :] = dc_r[a].astype(F32)
        ced[a, 56:64, :] = dk_r[2 * a + 1].astype(F32)[0:8]

    @pl.when(top)
    def _():
        ring_arrive(32, fd)
        total = jnp.zeros((32, 384), F32)
        for j in range(8):
            total += jnp.dot(fd[j], fold[j * 256 : (j + 1) * 256, :], preferred_element_type=F32)
        n = lax.broadcasted_iota(jnp.int32, (16, 384), 0)
        sign = jnp.where(n >= 2, -1.0, 1.0)
        for e in range(2):
            gd[e] = total[16 * (1 - e) : 16 * (2 - e)] * sign
            drf[1, 16 * e : 16 * e + 16, :] = gd[e][:, 0:256]

    @pl.when(jnp.logical_not(top))
    def _():
        gd[...] = jnp.zeros_like(gd)

    m = mext[...]
    for f, d in enumerate(forcing):
        third = unpacked(ced[0], ced[1], f)
        north = jnp.where(top, two_rows(0, gd[0, f : f + 1, 256:384], gd[1, f : f + 1, 256:384]), third[56:64])
        x = framed(
            d,
            two_rows(6, drf[0, f : f + 1, :], drf[0, 16 + f : 17 + f, :]),
            two_rows(0, drf[1, f : f + 1, :], drf[1, 16 + f : 17 + f, :]),
            jnp.concatenate([third[0:56], north], axis=0),
        )
        q = sea * step(m * step(x, 0.2), 0.2)[8:56, 0:256]
        q_out[f] = q
        if f == 0:
            c00 = jnp.concatenate([coef[0:1, :], coef[0:1, :]], axis=1)
            heat = sea * (xo[0, 0] + c00 * q)
            for h in range(2):
                fs[pl.ds(h, 48, stride=2), :] = heat[:, 128 * h : 128 * h + 128]
            sst_s[...] = fs[0:96, :].astype(BF)
            for dl, dn in around:
                n = 40 + direction[(dl, dn)]
                back = 40 + direction[(-dl, -dn)]
                slot = (1 - dl) * 3 + 1 - dn
                send_to(lat_ok(dn), sst_s, sst_r.at[slot], n, back, lon_at(dl), lat + dn)
    sst_r[4] = sst_s[...]
    for dl, dn in around:
        arrive(lat_ok(dn), sst_r.at[(1 + dl) * 3 + 1 + dn], 40 + direction[(dl, dn)])
    sst_out[...] = sst_r[...]
    for finish in pending:
        finish()
    ocean_out.wait()
    atm_out.wait()


def exchange(send, rows, cols, corn, atm, oce, mask, seam, mix_a, mix_o):
    here = pl.BlockSpec(memory_space=pltpu.VMEM)
    away = pl.BlockSpec(memory_space=pl.ANY)
    return pl.pallas_call(
        middle_kernel,
        in_specs=[away] * 6 + [here] * 4,
        out_specs=[away] * 2 + [here] * 4,
        out_shape=[
            jax.ShapeDtypeStruct((4, 16, 64, 256), F32),
            jax.ShapeDtypeStruct((4, 16, 48, 256), F32),
            jax.ShapeDtypeStruct((4, 48, 256), F32),
            jax.ShapeDtypeStruct((8, 48, 256), F32),
            jax.ShapeDtypeStruct((9, 96, 128), BF),
            jax.ShapeDtypeStruct((16, 128), F32),
        ],
        scratch_shapes=[
            pltpu.VMEM((4, 16, 64, 256), F32),
            pltpu.VMEM((4, 16, 48, 256), F32),
            pltpu.VMEM((4, 16, 64, 256), F32),
            pltpu.VMEM((4, 32, 48, 256), F32),
            pltpu.VMEM((3, 8, 96, 128), BF),
            pltpu.VMEM((3, 8, 96, 128), BF),
            pltpu.VMEM((3, 8, 96, 128), BF),
            pltpu.VMEM((2, 8, 96, 128), BF),
            pltpu.VMEM((2, 8, 96, 128), BF),
            pltpu.VMEM((2, 2, 144, 256), BF),
            pltpu.VMEM((2, 160, 128), BF),
            pltpu.VMEM((4, 32, 128), BF),
            pltpu.VMEM((8, 2, 80, 256), BF),
            pltpu.VMEM((2, 2, 144, 256), F32),
            pltpu.VMEM((2, 80, 128), F32),
            pltpu.VMEM((2, 64, 128), F32),
            pltpu.VMEM((2, 80, 128), F32),
            pltpu.VMEM((64, 384), F32),
            pltpu.VMEM((2048, 384), BF),
            pltpu.VMEM((2, 48, 256), F32),
            pltpu.VMEM((2, 256, 256), BF),
            pltpu.VMEM((2, 128, 256), BF),
            pltpu.VMEM((768, 128), F32),
            pltpu.VMEM((2, 32, 256), BF),
            pltpu.VMEM((2, 32, 256), BF),
            pltpu.VMEM((2, 48, 128), BF),
            pltpu.VMEM((2, 48, 128), BF),
            pltpu.VMEM((4, 16, 128), BF),
            pltpu.VMEM((8, 32, 256), BF),
            pltpu.VMEM((2, 32, 256), F32),
            pltpu.VMEM((2, 64, 128), F32),
            pltpu.VMEM((2, 16, 384), F32),
            pltpu.VMEM((96, 128), BF),
            pltpu.VMEM((9, 96, 128), BF),
            pltpu.SemaphoreType.DMA((6,)),
            pltpu.SemaphoreType.DMA((48,)),
            pltpu.SemaphoreType.DMA((48,)),
        ],
        compiler_params=pltpu.CompilerParams(collective_id=0, has_side_effects=True, vmem_limit_bytes=40 * MIB),
        name="exchange",
    )(send, rows, cols, corn, atm, oce, mask, seam, mix_a, mix_o)


BACK_STEPS = 8


def back_kernel(sst, dd, dt, q, coef, w, atm, oce, f_in, atm_out, ex, oce_out, f_out, sel, exs):
    i = pl.program_id(0)
    tiles = w.shape[0]
    fields = atm.shape[0]

    @pl.when(i == 0)
    def _():
        heat = sst[...].reshape(864, 128)
        for k in range(3):
            picked = lax.dot_general(one_hot_slots(dd, dt, k), heat, TN, preferred_element_type=F32)
            sel[k * 128 : (k + 1) * 128, :] = picked.astype(BF)

    row = lax.broadcasted_iota(jnp.int32, (16, 128), 0)
    even = (row & 1) == 0
    for g in range(tiles // 16):
        acc = jnp.zeros((16, 128), F32)
        t0 = pl.multiple_of(i * tiles + g * 16, 16)
        part = [sel[pl.ds(pl.multiple_of(k * 128 + t0, 16), 16), :] for k in range(3)]
        lhs = jnp.concatenate(part[:2], axis=1)
        last = part[2].astype(F32)
        split = jnp.concatenate([jnp.where(even, last, 0.0), jnp.where(even, 0.0, last)], axis=1).astype(BF)
        for j in range(0, 16, 4):
            n = g * 16 + j
            for h in range(2):
                p = n + 2 * h
                block = jnp.concatenate(
                    [jnp.concatenate([w[p, 0], w[p, 1]], axis=1), jnp.concatenate([w[p + 1, 0], w[p + 1, 1]], axis=1)],
                    axis=0,
                )
                r = lax.dot_general(lhs, block, NT, preferred_element_type=F32)
                acc += jnp.where(row == j + 2 * h, r[:, :128], 0.0) + jnp.where(row == j + 2 * h + 1, r[:, 128:], 0.0)
            block = jnp.concatenate(
                [jnp.concatenate([w[n, 2], w[n + 1, 2]], axis=1), jnp.concatenate([w[n + 2, 2], w[n + 3, 2]], axis=1)],
                axis=0,
            )
            r = lax.dot_general(split, block, NT, preferred_element_type=F32)
            acc += jnp.where((row == j) | (row == j + 1), r[:, :128], 0.0)
            acc += jnp.where((row == j + 2) | (row == j + 3), r[:, 128:], 0.0)
        exs[pl.ds(t0, 16), :] = acc

    atm_out[...] = atm[...]
    place = jnp.where(i < 5, i, jnp.where(i == 7, 5, i + 1))
    v = place // 2
    for j in range(fields):
        c = coef[pl.ds(lax.rem(place, 2) * fields + j, 1), :]
        oce_out[j] = oce[j] + jnp.concatenate([c, c], axis=1) * q[v]

    @pl.when(i == 0)
    def _():
        f_out[...] = f_in[...]

    @pl.when(i == pl.num_programs(0) - 1)
    def _():
        for h in range(2):
            at = slice(128 * h, 128 * h + 128)
            heat = exs[pl.ds(h, 64, stride=2), :]
            ex[:, at] = heat
            cold = atm[fields - 1, :, at]
            atm_out[fields - 1, :, at] = cold + 0.5 * (heat - cold)


def remap_back(sst, dd, dt, q, coef, w, atm, oce, flux):
    tiles = 128 // BACK_STEPS
    fields = 64 // BACK_STEPS
    whole = lambda *shape: pl.BlockSpec(shape, lambda i: (0,) * len(shape))
    place = lambda i: (jnp.where(i < 5, i, jnp.where(i == 7, 5, i + 1)), 0, 0)
    return pl.pallas_call(
        back_kernel,
        grid=(BACK_STEPS,),
        in_specs=[
            whole(9, 96, 128),
            whole(3, 128),
            whole(3, 128),
            whole(4, 48, 256),
            whole(16, 128),
            pl.BlockSpec((tiles, 3, 128, 128), lambda i: (i, 0, 0, 0)),
            pl.BlockSpec((fields, 64, 256), place),
            pl.BlockSpec((fields, 48, 256), place),
            whole(8, 48, 256),
        ],
        out_specs=[
            pl.BlockSpec((fields, 64, 256), place),
            whole(64, 256),
            pl.BlockSpec((fields, 48, 256), place),
            whole(8, 48, 256),
        ],
        out_shape=[
            jax.ShapeDtypeStruct((64, 64, 256), F32),
            jax.ShapeDtypeStruct((64, 256), F32),
            jax.ShapeDtypeStruct((64, 48, 256), F32),
            jax.ShapeDtypeStruct((8, 48, 256), F32),
        ],
        scratch_shapes=[pltpu.VMEM((384, 128), BF), pltpu.VMEM((128, 128), F32)],
        compiler_params=pltpu.CompilerParams(vmem_limit_bytes=40 * MIB),
        name="remap_back",
    )(sst, dd, dt, q, coef, w, atm.reshape(64, 64, 256), oce.reshape(64, 48, 256), flux)


def per_device(atmos, ts, sw, w, dd, dt, mix_a, ocean, mask, seam, mix_o):
    dd, dt = dd.T, dt.T
    send, rows, cols, corn = remap_out(atmos, ocean, ts, sw, w, dd, dt, mask)
    stepped, ss, q, flux, sst, coef = exchange(
        send, rows, cols, corn, atmos, ocean, mask, seam.reshape(1, 256), mix_a, mix_o
    )
    atm, ex, oce, flux = remap_back(sst, dd, dt, q, coef, w, stepped, ss, flux)
    return atm.reshape(atmos.shape), ex, oce.reshape(ocean.shape), flux


def solution(mesh):
    field = P(None, None, "lat", "lon")
    plane = P("lat", "lon")
    tiles = P(("lon", "lat"), None)
    return jax.shard_map(
        per_device,
        mesh=mesh,
        in_specs=(field, plane, plane, P(("lon", "lat"), None, None, None), tiles, tiles, P(), field, plane, P("lon"), P()),
        out_specs=(field, plane, field, P(None, "lat", "lon")),
        check_vma=False,
    )
```

profile of v0, /device:TPU:97, one launch (start us, length us, event | category | flops | bytes accessed | tf_op | source)
XLA Modules:
  0.0 109.9 jit_solution(17711399021583907097)
XLA Ops:
  0.6 0.0 copy-start
  0.6 2.2 %copy-done = f32[4,16,64,256]{3,2,1,0:T(8,128)S(1)} copy-done((f32[4,16,64,256]{3,2,1,0:T(8,128)S(1)}, f32[4,16,64,256]{3,2,1,0:T(8,128)}, u32[]{:S(2)}) %copy-start) | copy-done | bytes 4194328
  2.8 0.0 copy-start.1
  2.8 1.9 %copy-done.1 = f32[4,16,48,256]{3,2,1,0:T(8,128)S(1)} copy-done((f32[4,16,48,256]{3,2,1,0:T(8,128)S(1)}, f32[4,16,48,256]{3,2,1,0:T(8,128)}, u32[]{:S(2)}) %copy-start.1) | copy-done | bytes 3145752
  4.7 0.0 copy-start.3
  4.7 0.8 copy-done.3
  5.5 0.0 copy-start.5
  5.5 0.8 copy-done.5
  6.4 0.0 copy-start.6
  6.4 0.8 copy-done.6
  7.2 0.0 copy-start.9
  7.2 0.7 copy-done.9
  7.9 0.0 copy-start.10
  7.9 0.7 copy-done.10
  8.6 0.0 copy-start.2
  8.6 0.0 copy-start.4
  8.6 0.0 copy-start.7
  8.6 0.0 copy-start.8
  8.6 0.0 copy-start.11
  8.6 8.3 %remap_out.1 = (bf16[9,8,96,128]{3,2,1,0:T(8,128)(2,1)S(1)}, bf16[4,144,256]{2,1,0:T(8,128)(2,1)S(1)}, bf16[2,160,128]{2,1,0:T(8,128)(2,1)S(1)}, bf16[4,32,128]{2,1,0:T(8,128)(2,1)S(1)}) custom-call(f32[4,16,64,256]{3,2,1,0:T(8,128)S(1)} %copy-done, f32[64,256]{1,0:T(8,128)S(1)} %copy-done.5, f32[64,256]{1,0:T(8,128)S(1)} %copy-done.6, ...), custom_call_target="tpu_custom_call" | custom-call | tf_op jit(solution)/shard_map/remap_out/pallas_call | solution.py:137
  16.9 0.0 copy-done.2
  16.9 0.0 copy-done.4
  16.9 0.0 copy-done.7
  17.0 0.0 copy-done.8
  17.0 0.0 copy-done.11
  17.0 81.1 %exchange.1 = (f32[4,16,64,256]{3,2,1,0:T(8,128)S(1)}, f32[4,16,48,256]{3,2,1,0:T(8,128)S(1)}, f32[4,48,256]{2,1,0:T(8,128)S(1)}, f32[8,48,256]{2,1,0:T(8,128)S(...) custom-call(bf16[9,8,96,128]{3,2,1,0:T(8,128)(2,1)S(1)} %get-tuple-element.18.send, ...), custom_call_target="tpu_custom_call" | custom-call | tf_op jit(solution)/shard_map/exchange/pallas_call | solution.py:612
  98.1 11.9 %remap_back.1 = (f32[64,64,256]{2,1,0:T(8,128)}, f32[64,256]{1,0:T(8,128)}, f32[64,48,256]{2,1,0:T(8,128)}, f32[8,48,256]{2,1,0:T(8,128)}) custom-call(bf16[9,96,128]{2,1,0:T(8,128)(2,1)S(1)} %get-tuple-element.22.sst, s32[3,128]{1,0:T(4,128)S(1)} %bitcast.14, s32[3,128]{1,0:T(4,128)S(1)} %bitcast.16, f32[4,48,256]{2,1,0:T(8,128)S(1)} %get-tuple-element.23.q, ...), custom_call_target="tpu_custom_call" | custom-call | tf_op jit(solution)/shard_map/remap_back/pallas_call | solution.py:737
Async XLA Ops:
  0.6 2.2 %copy-start = (f32[4,16,64,256]{3,2,1,0:T(8,128)S(1)}, f32[4,16,64,256]{3,2,1,0:T(8,128)}, u32[]{:S(2)}) copy-start(f32[4,16,64,256]{3,2,1,0:T(8,128)} %atm.1) | copy-start | bytes 12582916
  2.8 1.9 %copy-start.1 = (f32[4,16,48,256]{3,2,1,0:T(8,128)S(1)}, f32[4,16,48,256]{3,2,1,0:T(8,128)}, u32[]{:S(2)}) copy-start(f32[4,16,48,256]{3,2,1,0:T(8,128)} %oce.1) | copy-start | bytes 9437188
  4.7 0.8 copy-start.3
  5.5 0.8 copy-start.5
  6.4 0.8 copy-start.6
  7.2 0.7 copy-start.9
  7.9 0.7 copy-start.10
  8.6 8.4 %copy-start.2 = (f32[4,16,48,256]{3,2,1,0:T(8,128)S(1)}, f32[4,16,48,256]{3,2,1,0:T(8,128)}, u32[]{:S(2)}) copy-start(f32[4,16,48,256]{3,2,1,0:T(8,128)} %oce.1) | copy-start | bytes 9437188
  8.6 8.4 %copy-start.4 = (s32[48,256]{1,0:T(8,128)S(1)}, s32[48,256]{1,0:T(8,128)}, u32[]{:S(2)}) copy-start(s32[48,256]{1,0:T(8,128)} %mask.3) | copy-start | bytes 147460
  8.6 8.4 %copy-start.7 = (f32[16,16]{1,0:T(8,128)S(1)}, f32[16,16]{1,0:T(8,128)}, u32[]{:S(2)}) copy-start(f32[16,16]{1,0:T(8,128)} %mix_a.1) | copy-start | bytes 3076
  8.6 8.4 %copy-start.8 = (f32[16,16]{1,0:T(8,128)S(1)}, f32[16,16]{1,0:T(8,128)}, u32[]{:S(2)}) copy-start(f32[16,16]{1,0:T(8,128)} %mix_o.1) | copy-start | bytes 3076
  8.6 8.4 %copy-start.11 = (s32[256]{0:T(256)S(1)}, s32[256]{0:T(256)}, u32[]{:S(2)}) copy-start(s32[256]{0:T(256)} %param.20) | copy-start | bytes 3076
where the time goes:
time: 111 us; the launch traced here: 110 us
  Pallas kernels  101 us (91%)
  local copies, waits for them, and re-layouts  7.93 us (7%)
    pallas_call x1, Pallas kernels, exchange(): pl.pallas_call(middle_kernel, in_specs=[away] * 6 + [here] * 4, out_specs...  81.1 us
    pallas_call x1, Pallas kernels, remap_back(): pl.pallas_call(back_kernel, grid=(BACK_STEPS,), in_specs=[whole(9, 96, 12...  11.9 us
    pallas_call x1, Pallas kernels, remap_out(): pl.pallas_call(out_kernel, grid=(STEPS,), in_specs=[pl.BlockSpec((4, 1, 6...  8.34 us
    unnamed x24, local copies, waits for them, and re-layouts  7.93 us

commit v1 on v0

v1 whole, which is shorter than its diff:
```python
import functools

import jax
import jax.numpy as jnp
from jax import lax
from jax.experimental import pallas as pl
from jax.experimental.pallas import tpu as pltpu
from jax.sharding import PartitionSpec as P

F32 = jnp.float32
BF = jnp.bfloat16
MESH = pl.DeviceIdType.MESH
HIGHEST = lax.Precision.HIGHEST
NT = (((1,), (1,)), ((), ()))
TN = (((0,), (0,)), ((), ()))
N_LON = 8
N_LAT = 16
CHUNKS = 8
MIB = 2**20


def flux_fields(u, v, ta, qa, ts, sw):
    speed = jnp.sqrt(u * u + v * v + 1.0)
    soft = jnp.maximum(qa, 0.0) + jnp.log1p(jnp.exp(-jnp.abs(qa)))
    return [
        0.8 * speed * u,
        0.8 * speed * v,
        0.6 * speed * (ts - ta),
        0.5 * speed * (0.4 * jnp.exp(0.5 * ts) - qa),
        0.3 * (ta - ts) * (2.0 + jnp.tanh(ta)),
        sw * (0.9 - 0.1 * jnp.tanh(qa)),
        soft,
        0.3 * speed * speed,
    ]


def slot_rows(owner, tile):
    lon = lax.axis_index("lon")
    lat = lax.axis_index("lat")
    lon_offset = ((owner >> 4) - lon + 1) & 7
    lat_offset = (owner & 15) - lat + 1
    return (lon_offset * 3 + lat_offset) * 96 + tile


def one_hot_slots(dd, dt, k):
    slot = slot_rows(dd[k : k + 1, :], dt[k : k + 1, :])
    rows = lax.broadcasted_iota(jnp.int32, (864, 128), 0)
    return jnp.where(slot == rows, 1.0, 0.0).astype(BF)


def out_kernel(
    atm, oce, ts, sw, dd_far, dt_far, mask_far, w,
    send, rows, cols, corn, atm_here, oce_here, w_here,
    surf, heat, sun, dd, dt, mask, ft, terms, oh, tb, rbuf, sem,
):
    chunk = 128 // CHUNKS
    copies = [
        pltpu.make_async_copy(atm.at[:, 15], surf, sem.at[0]),
        pltpu.make_async_copy(ts, heat, sem.at[1]),
        pltpu.make_async_copy(sw, sun, sem.at[2]),
        pltpu.make_async_copy(mask_far, mask, sem.at[5 + CHUNKS]),
    ]
    targets = [
        pltpu.make_async_copy(dd_far, dd, sem.at[6 + CHUNKS]),
        pltpu.make_async_copy(dt_far, dt, sem.at[7 + CHUNKS]),
    ]
    for copy in targets:
        copy.start()
    weights = lambda i: pltpu.make_async_copy(
        w.at[pl.ds(i * chunk, chunk)], w_here.at[pl.ds(i * chunk, chunk)], sem.at[3 + i]
    )
    fields = [
        pltpu.make_async_copy(atm, atm_here, sem.at[3 + CHUNKS]),
        pltpu.make_async_copy(oce, oce_here, sem.at[4 + CHUNKS]),
    ]
    for copy in copies:
        copy.start()
    for i in range(CHUNKS):
        weights(i).start()
    for copy in fields:
        copy.start()

    for copy in targets:
        copy.wait()
    for k in range(3):
        oh[:, k * 128 : (k + 1) * 128] = one_hot_slots(dd, dt, k)
    for copy in copies:
        copy.wait()
    for f, val in enumerate(flux_fields(surf[0], surf[1], surf[2], surf[3], heat[...], sun[...])):
        val = val.astype(BF).astype(F32)
        ft[pl.ds(f, 64, stride=16), :] = val[:, :128]
        ft[pl.ds(8 + f, 64, stride=16), :] = val[:, 128:]

    group = lax.broadcasted_iota(jnp.int32, (32, 128), 0)
    even = (group & 8) == 0

    @pl.loop(0, CHUNKS)
    def _(i):
        weights(i).wait()
        for j in range(0, chunk, 4):
            t = i * chunk + j
            a = ft[pl.ds(pl.multiple_of(t * 8, 32), 32), :]
            lhs = jnp.concatenate([jnp.where(even, a, 0.0), jnp.where(even, 0.0, a)], axis=1).astype(BF)
            quad = [[w_here[t + q, k] for k in range(3)] for q in range(4)]
            for h in range(2):
                p, q = quad[2 * h], quad[2 * h + 1]
                block = jnp.concatenate([jnp.concatenate(p[:2], axis=1), jnp.concatenate(q[:2], axis=1)], axis=0)
                r = jnp.dot(lhs[16 * h : 16 * h + 16], block, preferred_element_type=F32)
                for k in range(2):
                    terms[pl.ds(pl.multiple_of((k * 128 + t + 2 * h) * 8, 16), 16), :] = r[:, k * 128 : (k + 1) * 128]
            block = jnp.concatenate(
                [
                    jnp.concatenate([quad[0][2], quad[2][2]], axis=1),
                    jnp.concatenate([quad[1][2], quad[3][2]], axis=1),
                ],
                axis=0,
            )
            r = jnp.dot(lhs, block, preferred_element_type=F32)
            at = pl.multiple_of((256 + t) * 8, 32)
            terms[pl.ds(at, 16), :] = r[:16, :128]
            terms[pl.ds(at + 16, 16), :] = r[16:, 128:]

    for copy in fields:
        copy.wait()
    lane_a = lax.broadcasted_iota(jnp.int32, (64, 128), 1) >> 1
    lane_o = lax.broadcasted_iota(jnp.int32, (48, 128), 1) >> 1
    za = jnp.zeros((64, 128), F32)
    zo = jnp.zeros((48, 128), F32)

    @pl.loop(0, 16, init_carry=(za, za, zo, zo))
    def packed(l, carry):
        left_a, right_a, left_o, right_o = carry
        for v in range(4):
            n = v * 16 + l
            ahead = 2 * n
            back = (2 * n + 2) & 127
            left_a = jnp.where(lane_a == n, pltpu.roll(atm_here[v, l, :, 0:128], ahead, 1), left_a)
            right_a = jnp.where(lane_a == n, pltpu.roll(atm_here[v, l, :, 128:256], back, 1), right_a)
            left_o = jnp.where(lane_o == n, pltpu.roll(oce_here[v, l, :, 0:128], ahead, 1), left_o)
            right_o = jnp.where(lane_o == n, pltpu.roll(oce_here[v, l, :, 128:256], back, 1), right_o)
            for e in range(2):
                rbuf[e, pl.ds(n, 1), :] = atm_here[v, l, e : e + 1, :]
                rbuf[2 + e, pl.ds(n, 1), :] = atm_here[v, l, 62 + e : 63 + e, :]
                rbuf[e, pl.ds(64 + n, 1), :] = oce_here[v, l, e : e + 1, :]
                rbuf[2 + e, pl.ds(64 + n, 1), :] = oce_here[v, l, 46 + e : 47 + e, :]
        return left_a, right_a, left_o, right_o

    sea = mask[...].astype(F32)
    for side in range(2):
        cols_a, cols_o = packed[side], packed[2 + side]
        cols[side, 0:64, :] = cols_a.astype(BF)
        cols[side, 64:112, :] = cols_o.astype(BF)
        cols[side, 112:160, :] = sea[:, 128 * side : 128 * side + 128].astype(BF)
        corn[2 * side, 0:16, :] = cols_a[0:16].astype(BF)
        corn[2 * side, 16:32, :] = cols_o[0:16].astype(BF)
        corn[2 * side + 1, 0:16, :] = cols_a[48:64].astype(BF)
        corn[2 * side + 1, 16:32, :] = cols_o[32:48].astype(BF)
    for e in range(2):
        for b in range(2):
            r = 46 * b + e
            rbuf[2 * b + e, 128:144, :] = jnp.broadcast_to(sea[r : r + 1, :], (16, 256))
    rows[...] = rbuf[...].astype(BF)

    for f in range(8):
        tb[:, f * 128 : (f + 1) * 128] = terms[pl.ds(f, 384, stride=8), :].astype(BF)
    for g in range(4):
        res = jnp.dot(oh[...], tb[:, g * 256 : (g + 1) * 256], preferred_element_type=F32)
        for o in range(9):
            for b in range(2):
                send[o, 2 * g + b] = res[o * 96 : (o + 1) * 96, b * 128 : (b + 1) * 128].astype(BF)


HERE = pl.BlockSpec(memory_space=pltpu.VMEM)
AWAY = pl.BlockSpec(memory_space=pltpu.HBM)


def remap_out(atm, oce, ts, sw, w, dd, dt, mask):
    return pl.pallas_call(
        out_kernel,
        in_specs=[AWAY] * 8,
        out_specs=[HERE] * 7,
        out_shape=[
            pltpu.VMEM((9, 8, 96, 128), BF),
            pltpu.VMEM((4, 144, 256), BF),
            pltpu.VMEM((2, 160, 128), BF),
            pltpu.VMEM((4, 32, 128), BF),
            pltpu.VMEM((4, 16, 64, 256), F32),
            pltpu.VMEM((4, 16, 48, 256), F32),
            pltpu.VMEM((128, 3, 128, 128), BF),
        ],
        scratch_shapes=[
            pltpu.VMEM((4, 64, 256), F32),
            pltpu.VMEM((64, 256), F32),
            pltpu.VMEM((64, 256), F32),
            pltpu.VMEM((3, 128), jnp.int32),
            pltpu.VMEM((3, 128), jnp.int32),
            pltpu.VMEM((48, 256), jnp.int32),
            pltpu.VMEM((1024, 128), F32),
            pltpu.VMEM((3072, 128), F32),
            pltpu.VMEM((864, 384), BF),
            pltpu.VMEM((384, 1024), BF),
            pltpu.VMEM((4, 144, 256), F32),
            pltpu.SemaphoreType.DMA((8 + CHUNKS,)),
        ],
        compiler_params=pltpu.CompilerParams(vmem_limit_bytes=16 * MIB),
        name="remap_out",
    )(*[pltpu.with_memory_space_constraint(x, pltpu.HBM) for x in (atm, oce, ts, sw, dd, dt, mask, w)])


def step(x, rate):
    rows, lanes = x.shape
    around = pltpu.roll(x, 1, 0) + pltpu.roll(x, rows - 1, 0) + pltpu.roll(x, 1, 1) + pltpu.roll(x, lanes - 1, 1)
    return (1.0 - 4.0 * rate) * x + rate * around


def step_from(x, around, rate):
    return (1.0 - 4.0 * rate) * x + rate * around


def unpacked(from_left, from_right, n):
    lane = lax.broadcasted_iota(jnp.int32, from_left.shape, 1)
    right = pltpu.roll(from_right, (128 - 2 * n) & 127, 1)
    left = pltpu.roll(from_left, 126 - 2 * n, 1)
    return jnp.where(lane < 2, right, jnp.where(lane >= 126, left, 0.0))


def two_rows(at, first, second):
    rows = lax.broadcasted_iota(jnp.int32, (8, first.shape[1]), 0)
    return jnp.where(rows == at, first, jnp.where(rows == at + 1, second, 0.0))


def framed(x, south, north, third):
    return jnp.concatenate([jnp.concatenate([south, x, north], axis=0), third], axis=1)


def lateral(parts, tri):
    rows = parts[0].shape[0]
    total = jnp.dot(jnp.concatenate(parts, axis=0).astype(BF), tri, preferred_element_type=F32)
    return [total[n * rows : (n + 1) * rows] for n in range(len(parts))]


def near(x, inner, above, below, ghost):
    rows = x.shape[0]
    lane = lax.broadcasted_iota(jnp.int32, (rows, 128), 1)
    row = lax.broadcasted_iota(jnp.int32, (8, 256), 0)
    up = pltpu.roll(x, 1, 0)
    down = pltpu.roll(x, rows - 1, 0)
    up = jnp.concatenate([jnp.where(row == 0, above, up[0:8]), up[8:]], axis=0)
    down = jnp.concatenate([down[: rows - 8], jnp.where(row == 7, below, down[rows - 8 :])], axis=0)
    edges = jnp.concatenate([jnp.where(lane == 0, ghost, 0.0), jnp.where(lane == 127, ghost, 0.0)], axis=1)
    return up + down + inner + edges


def beside(x, ghost, lane):
    t0, t1 = x[:, 0:128], x[:, 128:256]
    r0, r1 = pltpu.roll(t0, 1, 1), pltpu.roll(t1, 1, 1)
    l0, l1 = pltpu.roll(t0, 127, 1), pltpu.roll(t1, 127, 1)
    first, last = lane == 0, lane == 127
    s0 = jnp.where(first, ghost, r0) + jnp.where(last, l1, l0)
    s1 = jnp.where(first, r0, r1) + jnp.where(last, ghost, l1)
    return jnp.concatenate([s0, s1], axis=1)


def beside_packed(left, right, own_left, own_right, odd):
    centre = jnp.where(odd, left, right)
    outer = jnp.where(odd, pltpu.roll(left, 1, 1), pltpu.roll(right, 127, 1))
    inner = jnp.where(odd, pltpu.roll(own_left, 1, 1), pltpu.roll(own_right, 127, 1))
    return centre, outer + inner


def corner_lanes(centre, row):
    lane = lax.broadcasted_iota(jnp.int32, (64, 128), 1)
    field = lax.broadcasted_iota(jnp.int32, (64, 128), 0)
    line = jnp.broadcast_to(centre[row : row + 1, :], (64, 128))
    left = jnp.sum(jnp.where(lane == 2 * field + 1, line, 0.0), axis=1, keepdims=True)
    right = jnp.sum(jnp.where(lane == 2 * field, line, 0.0), axis=1, keepdims=True)
    return jnp.where(lane == 0, left, jnp.where(lane == 127, right, 0.0))


def spread(mixer, cells):
    size = 16 * cells
    pick = lambda dim: jnp.where(
        lax.broadcasted_iota(jnp.int32, (size, 16) if dim == 0 else (16, size), dim) // cells
        == lax.broadcasted_iota(jnp.int32, (size, 16) if dim == 0 else (16, size), 1 - dim),
        1.0,
        0.0,
    )
    dot = functools.partial(jnp.dot, precision=HIGHEST, preferred_element_type=F32)
    full = dot(dot(pick(0), mixer), pick(1))
    r = lax.broadcasted_iota(jnp.int32, (size, size), 0) % cells
    c = lax.broadcasted_iota(jnp.int32, (size, size), 1) % cells
    return jnp.where(r == c, full, 0.0)


def halves(x):
    high = x.astype(BF)
    return high, (x - high.astype(F32)).astype(BF)


def dot3(lhs_high, lhs_low, x):
    high, low = halves(x)
    dot = functools.partial(jnp.dot, preferred_element_type=F32)
    return dot(lhs_high, high) + dot(lhs_high, low) + dot(lhs_low, high)


def middle_kernel(
    send, rows, cols, corn, atm, oce, mask, seam, mix_a, mix_o,
    stepped, ss, q_out, f_out, sst_out, coef_out,
    lla, bc, pr, ro, rl, sl, rr, cc, kk, fr, rrf, cea, ceo, mext, fold, gsa, gso, gea, geo, tri,
    ka, ko, fs, dr_s, dr_r, dc_s, dc_r, dk_r, fd, drf, ced, gd, sst_s, sst_r,
    lsem, ssem, rsem,
):
    lon = lax.axis_index("lon")
    lat = lax.axis_index("lat")
    side = lax.rem(lat, 2)
    partner = lat + 1 - 2 * side
    outer = lat - 1 + 2 * side
    has_outer = jnp.logical_and(outer >= 0, outer < N_LAT)
    has_south = lat > 0
    has_north = lat < N_LAT - 1
    top = lat == N_LAT - 1
    always = lat >= 0
    lon_at = lambda d: lax.rem(lon + d + N_LON, N_LON)

    def lat_ok(d):
        return always if d == 0 else (has_south if d < 0 else has_north)

    def send_to(cond, src, dst, n, m, dev_lon, dev_lat):
        copy = pltpu.make_async_remote_copy(
            src_ref=src, dst_ref=dst, send_sem=ssem.at[n], recv_sem=rsem.at[m],
            device_id=(dev_lon, dev_lat), device_id_type=MESH,
        )

        @pl.when(cond)
        def _():
            copy.start()

        def finish():
            @pl.when(cond)
            def _():
                copy.wait_send()

        pending.append(finish)

    def arrive(cond, dst, m):
        @pl.when(cond)
        def _():
            pltpu.make_async_remote_copy(
                src_ref=dst, dst_ref=dst, send_sem=ssem.at[0], recv_sem=rsem.at[m],
                device_id=(lon, partner), device_id_type=MESH,
            ).wait_recv()

    pending = []
    barrier = pltpu.get_barrier_semaphore()
    around = [(dl, dn) for dl in (-1, 0, 1) for dn in (-1, 0, 1) if (dl, dn) != (0, 0)]
    for dl, dn in around:

        @pl.when(lat_ok(dn))
        def _(dl=dl, dn=dn):
            pl.semaphore_signal(barrier, inc=1, device_id=(lon_at(dl), lat + dn), device_id_type=MESH)

    @pl.when(top)
    def _():
        for d in range(2, N_LON - 1):
            pl.semaphore_signal(barrier, inc=1, device_id=(lon_at(d), lat), device_id_type=MESH)
        pl.semaphore_wait(barrier, 5 + 5)

    @pl.when(lat == 0)
    def _():
        pl.semaphore_wait(barrier, 5)

    @pl.when(jnp.logical_and(has_south, has_north))
    def _():
        pl.semaphore_wait(barrier, 8)

    direction = {pair: n for n, pair in enumerate(around)}

    def halo(first, rows_s, rows_r, cols_s, cols_r, corn_s, corn_r):
        for dl, dn in around:
            n = first + direction[(dl, dn)]
            back = first + direction[(-dl, -dn)]
            if dl == 0:
                src, dst = rows_s(max(dn, 0)), rows_r(max(-dn, 0))
            elif dn == 0:
                src, dst = cols_s(max(dl, 0)), cols_r(max(-dl, 0))
            else:
                src, dst = corn_s(max(dl, 0), max(dn, 0)), corn_r(max(-dl, 0), max(-dn, 0))
            send_to(lat_ok(dn), src, dst, n, back, lon_at(dl), lat + dn)

    def halo_arrive(first, rows_r, cols_r, corn_r):
        for dl, dn in around:
            n = first + direction[(dl, dn)]
            if dl == 0:
                dst = rows_r(max(dn, 0))
            elif dn == 0:
                dst = cols_r(max(dl, 0))
            else:
                dst = corn_r(max(dl, 0), max(dn, 0))
            arrive(lat_ok(dn), dst, n)

    def ring(first, src, landing):
        for d in range(1, N_LON):
            send_to(top, src, landing.at[lon], first + d, first + lon, lon_at(d), lat)

    def ring_arrive(first, landing):
        for d in range(1, N_LON):
            arrive(top, landing.at[lon_at(d)], first + lon_at(d))

    rows_r = lambda b: rr.at[b]
    cols_r = lambda a: cc.at[a]
    corn_r = lambda a, b: kk.at[2 * a + b]
    halo(0, lambda b: rows.at[pl.ds(2 * b, 2)], rows_r, lambda a: cols.at[a], cols_r, lambda a, b: corn.at[2 * a + b], corn_r)
    fold_src = rows.at[pl.ds(2, 2), pl.ds(64, 80)]
    ring(8, fold_src, fr)
    own_fold = pltpu.make_async_copy(fold_src, fr.at[lon], lsem.at[0])

    @pl.when(top)
    def _():
        own_fold.start()

    for dl in (0, 2, 1):
        send_to(always, send.at[dl * 3 + 2 - 2 * side], pr.at[dl], 16 + dl, 16 + dl, lon, partner)
    for dl in range(3):
        send_to(has_outer, send.at[dl * 3 + 2 * side], ro.at[dl], 19 + dl, 19 + dl, lon_at(dl - 1), outer)

    @pl.when(jnp.logical_not(has_outer))
    def _():
        ro[...] = jnp.zeros_like(ro)

    for b, cond in ((0, has_south), (1, has_north)):

        @pl.when(jnp.logical_not(cond))
        def _(b=b):
            rr[b] = jnp.zeros(rr.shape[1:], BF)
            dr_r[b] = jnp.zeros(dr_r.shape[1:], BF)
            for a in range(2):
                kk[2 * a + b] = jnp.zeros(kk.shape[1:], BF)
                dk_r[2 * a + b] = jnp.zeros(dk_r.shape[1:], BF)
            for dl in range(3):
                sst_r[dl * 3 + 2 * b] = jnp.zeros(sst_r.shape[1:], BF)

    for dl in (0, 2, 1):
        arrive(always, pr.at[dl], 16 + dl)
    for n, dl in enumerate((0, 2)):

        @pl.loop(0, 8)
        def _(f, n=n, dl=dl):
            sl[n, f] = (send[3 * dl + 1, f].astype(F32) + pr[dl, f].astype(F32)).astype(BF)

        send_to(always, sl.at[n], rl.at[n], 22 + n, 22 + n, lon_at(dl - 1), lat)

    ma = mix_a[...]
    mo = mix_o[...]
    dot = functools.partial(jnp.dot, precision=HIGHEST, preferred_element_type=F32)
    ma2 = dot(ma, ma)
    mo2 = dot(mo, mo)
    ka[0], ka[1] = halves(spread(ma2, 16))
    ko[0, :, 0:128], ko[1, :, 0:128] = halves(spread(mo2, 8))
    ko[0, :, 128:256], ko[1, :, 128:256] = halves(spread(mo, 8))
    coef = jnp.broadcast_to(mo2[:, 0:1], (16, 128))
    coef_out[...] = coef

    @pl.when(top)
    def _():
        lane = lax.broadcasted_iota(jnp.int32, (1, 384), 1)
        column = lon * 256 + jnp.where(lane < 320, lane, lane - 384)
        pole = seam[0:1, 0:1] + lon * 256
        source = (pole - column) & 2047
        for j in range(8):
            fold[j * 256 : (j + 1) * 256, :] = jnp.where(
                lax.broadcasted_iota(jnp.int32, (256, 384), 0) + j * 256 == source, 1.0, 0.0
            ).astype(BF)

    halo_arrive(0, rows_r, cols_r, corn_r)
    for b in range(2):
        for e in range(2):
            rrf[b, e] = rr[b, e].astype(F32)
    for a in range(2):
        side_cols = cc[a].astype(F32)
        ks = kk[2 * a].astype(F32)
        kn = kk[2 * a + 1].astype(F32)
        cea[a, 0:8, :] = ks[8:16]
        cea[a, 8:72, :] = side_cols[0:64]
        cea[a, 72:80, :] = kn[0:8]
        ceo[a, 0:8, :] = ks[24:32]
        ceo[a, 8:56, :] = side_cols[64:112]
        ceo[a, 56:64, :] = kn[16:24]

    @pl.when(top)
    def _():
        own_fold.wait()
        ring_arrive(8, fr)
        total = jnp.zeros((160, 384), F32)
        for j in range(8):
            total += jnp.dot(fr[j].reshape(160, 256), fold[j * 256 : (j + 1) * 256, :], preferred_element_type=F32)
        n = lax.broadcasted_iota(jnp.int32, (80, 384), 0)
        sign = jnp.where(jnp.logical_and(n >= 32, n < 64), -1.0, 1.0)
        for e in range(2):
            ghost = total[80 * (1 - e) : 80 * (2 - e)] * sign
            if e == 0:
                beyond = ghost[0:64, 256:384]
            rrf[1, e, 64:144, :] = ghost[:, 0:256]
        lane = lax.broadcasted_iota(jnp.int32, (64, 128), 1)
        field = lax.broadcasted_iota(jnp.int32, (64, 128), 0)
        both = jnp.where(lane == 2 * field + 1, beyond[:, 127:128], jnp.where(lane == 2 * field, beyond[:, 0:1], 0.0))
        both = jnp.sum(both, axis=0, keepdims=True)
        ceo[0, 56:57, :] = both
        ceo[1, 56:57, :] = both

    lane_m = lax.broadcasted_iota(jnp.int32, (48, 128), 1)
    sea = mask[...].astype(F32)
    sea_left = cc[0, 112:160, :].astype(F32)
    sea_right = cc[1, 112:160, :].astype(F32)
    third = jnp.where(lane_m < 2, sea_right, jnp.where(lane_m >= 126, sea_left, 0.0))
    none = jnp.zeros((8, 128), F32)
    mext[...] = framed(
        sea,
        two_rows(6, rrf[0, 0, 128:129, :], rrf[0, 1, 128:129, :]),
        two_rows(0, rrf[1, 0, 128:129, :], rrf[1, 1, 128:129, :]),
        jnp.concatenate([none, third, none], axis=0),
    )
    lane_f = lax.broadcasted_iota(jnp.int32, (64, 128), 1)

    def outside(ce, own_at, rows, at, rate, sea_side, sea_rows):
        odd = (lax.broadcasted_iota(jnp.int32, (rows + 16, 128), 1) & 1) == 1
        own = [
            jnp.concatenate([none, cols[a, own_at : own_at + rows, :].astype(F32), none], axis=0)
            for a in range(2)
        ]
        centre, lateral = beside_packed(ce[0], ce[1], own[0], own[1], odd)
        y = step_from(centre, pltpu.roll(centre, 1, 0) + pltpu.roll(centre, rows + 15, 0) + lateral, rate)
        x_side, y_side = centre[8 : 8 + rows], y[8 : 8 + rows]
        pack = lambda x: pltpu.roll(x, 127, 1)
        sides = [pack(x_side), pack(y_side if sea_side is None else y_side * sea_side)]
        if sea_side is not None:
            sides.append(pack(x_side - x_side * sea_side))
        ends = []
        for b in range(2):
            near_row = rrf[b, 1 - b, at : at + 64, :]
            far_row = rrf[b, b, at : at + 64, :]
            own_row = rows_in[2 * b + b, at : at + 64, :].astype(F32)
            ghost = corner_lanes(centre, 7 if b == 0 else rows + 8)
            z = step_from(near_row, far_row + own_row + beside(near_row, ghost, lane_f), rate)
            if sea_side is None:
                ends.append([jnp.where(has_south if b == 0 else has_north, z, 0.0)])
            else:
                ends.append([z * sea_rows[b], near_row - near_row * sea_rows[b]])
        return sides, ends

    rows_in = rows
    odd_m = (lane_m & 1) == 1
    sea_side = jnp.where(odd_m, jnp.broadcast_to(sea_left[:, 127:128], (48, 128)), jnp.broadcast_to(sea_right[:, 0:1], (48, 128)))
    sides, ends = outside(ceo, 64, 48, 64, 0.2, sea_side, [rrf[0, 1, 128:129, :], rrf[1, 0, 128:129, :]])
    for n in range(3):
        gso[n] = sides[n]
    for b in range(2):
        for n in range(2):
            geo[b, n] = ends[b][n]
    sides, ends = outside(cea, 0, 64, 0, 0.15, None, None)
    for n in range(2):
        gsa[n] = sides[n]
    for b in range(2):
        gea[b] = ends[b][0]

    r256 = lax.broadcasted_iota(jnp.int32, (256, 256), 0)
    c256 = lax.broadcasted_iota(jnp.int32, (256, 256), 1)
    tri[...] = jnp.where(jnp.logical_or(r256 == c256 + 1, r256 + 1 == c256), 1.0, 0.0).astype(BF)

    @pl.loop(0, 8)
    def _(i):
        v = i // 2
        first = pl.multiple_of(lax.rem(i, 2) * 8, 8)
        lines = pl.ds(pl.multiple_of(i * 8, 8), 8)
        far = pl.ds(pl.multiple_of(64 + i * 8, 8), 8)
        turned = lambda k, j: pltpu.roll(gso[k], (128 - 2 * (i * 8 + j)) & 127, 1)
        wet_here = mext[8:56, 0:256]
        south, north = rrf[0, 1, far, :], rrf[1, 0, far, :]
        xs = [oce[v, first + j] for j in range(8)]
        inner = lateral(xs, tri[...])
        a, c = [], []
        for j, x in enumerate(xs):
            around = near(x, inner[j], south[j : j + 1], north[j : j + 1], turned(0, j))
            a.append(wet_here * step_from(x, around, 0.2))
            c.append(x - wet_here * x)
        for k, parts in enumerate((a, c)):
            inner = lateral(parts, tri[...])
            south, north = geo[0, k, lines, :], geo[1, k, lines, :]
            for j, x in enumerate(parts):
                around = near(x, inner[j], south[j : j + 1], north[j : j + 1], turned(1 + k, j))
                bc[v, 16 * k + first + j] = step_from(x, around, 0.2)

    @pl.loop(0, 24, unroll=3)
    def _(n):
        v = n // 6
        at = pl.multiple_of(lax.rem(n, 6) * 8, 8)
        mixed = dot3(ko[0], ko[1], bc[v, :, pl.ds(at, 8), :].reshape(256, 256)).reshape(16, 8, 256)
        wet = mask[pl.ds(at, 8), :] > 0
        ss[v, :, pl.ds(at, 8), :] = jnp.where(wet[None], mixed, oce[v, :, pl.ds(at, 8), :])

    @pl.loop(0, 8)
    def _(i):
        v = i // 2
        first = pl.multiple_of(lax.rem(i, 2) * 8, 8)
        lines = pl.ds(pl.multiple_of(i * 8, 8), 8)
        turned = lambda k, j: pltpu.roll(gsa[k], (128 - 2 * (i * 8 + j)) & 127, 1)
        parts = [atm[v, first + j] for j in range(8)]
        ends = ((rrf[0, 1, lines, :], rrf[1, 0, lines, :]), (gea[0, lines, :], gea[1, lines, :]))
        for k in range(2):
            inner = lateral(parts, tri[...])
            south, north = ends[k]
            parts = [
                step_from(x, near(x, inner[j], south[j : j + 1], north[j : j + 1], turned(k, j)), 0.15)
                for j, x in enumerate(parts)
            ]
        for j, y in enumerate(parts):
            lla[v, first + j] = y

    @pl.loop(0, 16, unroll=4)
    def _(n):
        v = n // 4
        at = pl.multiple_of(lax.rem(n, 4) * 16, 16)
        mixed = dot3(ka[0], ka[1], lla[v, :, pl.ds(at, 16), :].reshape(256, 256))
        stepped[v, :, pl.ds(at, 16), :] = mixed.reshape(16, 16, 256)

    for dl in range(3):
        arrive(has_outer, ro.at[dl], 19 + dl)
    for n in range(2):
        arrive(always, rl.at[n], 22 + n)

    @pl.loop(0, 8)
    def _(f):
        parts = [send[4, f], pr[1, f], rl[0, f], rl[1, f], ro[0, f], ro[1, f], ro[2, f]]
        total = functools.reduce(lambda x, y: x + y, [p.astype(F32) for p in parts])
        fs[pl.ds(pl.multiple_of(f * 96, 8), 96), :] = total

    flux = []
    for f in range(8):
        value = sea * jnp.concatenate([fs[pl.ds(f * 96 + h, 48, stride=2), :] for h in range(2)], axis=1)
        f_out[f] = value
        flux.append(value)
    forcing = [
        0.2 * sea * (flux[5] - flux[2] - flux[3] - flux[4]),
        0.2 * sea * (flux[3] - flux[6]),
        sea * (0.3 * flux[0] - 0.1 * flux[7] * oce[2, 0]),
        sea * (0.3 * flux[1] - 0.1 * flux[7] * oce[3, 0]),
    ]

    left = jnp.zeros((48, 128), F32)
    right = jnp.zeros((48, 128), F32)
    edge = [[jnp.zeros((16, 256), F32) for _ in range(2)] for _ in range(2)]
    row_16 = lax.broadcasted_iota(jnp.int32, (16, 256), 0)
    for f, d in enumerate(forcing):
        left = jnp.where((lane_m >> 1) == f, pltpu.roll(d[:, 0:128], 2 * f, 1) if f else d[:, 0:128], left)
        right = jnp.where((lane_m >> 1) == f, pltpu.roll(d[:, 128:256], 2 * f + 2, 1), right)
        for b in range(2):
            for e in range(2):
                r = 46 * b + e
                edge[b][e] = jnp.where(row_16 == f, d[r : r + 1, :], edge[b][e])
    dc_s[0] = left.astype(BF)
    dc_s[1] = right.astype(BF)
    for b in range(2):
        for e in range(2):
            dr_s[b, 16 * e : 16 * e + 16, :] = edge[b][e].astype(BF)
    rows_r = lambda b: dr_r.at[b]
    cols_r = lambda a: dc_r.at[a]
    corn_r = lambda a, b: dk_r.at[2 * a + b]
    halo(24, lambda b: dr_s.at[b], rows_r, lambda a: dc_s.at[a], cols_r,
         lambda a, b: dc_s.at[a, pl.ds(32 * b, 16)], corn_r)
    ring(32, dr_s.at[1], fd)

    @pl.when(top)
    def _():
        fd[lon] = dr_s[1]

    halo_arrive(24, rows_r, cols_r, corn_r)
    for b in range(2):
        drf[b] = dr_r[b].astype(F32)
    for a in range(2):
        ced[a, 0:8, :] = dk_r[2 * a].astype(F32)[8:16]
        ced[a, 8:56, :] = dc_r[a].astype(F32)
        ced[a, 56:64, :] = dk_r[2 * a + 1].astype(F32)[0:8]

    @pl.when(top)
    def _():
        ring_arrive(32, fd)
        total = jnp.zeros((32, 384), F32)
        for j in range(8):
            total += jnp.dot(fd[j], fold[j * 256 : (j + 1) * 256, :], preferred_element_type=F32)
        n = lax.broadcasted_iota(jnp.int32, (16, 384), 0)
        sign = jnp.where(n >= 2, -1.0, 1.0)
        for e in range(2):
            gd[e] = total[16 * (1 - e) : 16 * (2 - e)] * sign
            drf[1, 16 * e : 16 * e + 16, :] = gd[e][:, 0:256]

    @pl.when(jnp.logical_not(top))
    def _():
        gd[...] = jnp.zeros_like(gd)

    m = mext[...]
    for f, d in enumerate(forcing):
        third = unpacked(ced[0], ced[1], f)
        north = jnp.where(top, two_rows(0, gd[0, f : f + 1, 256:384], gd[1, f : f + 1, 256:384]), third[56:64])
        x = framed(
            d,
            two_rows(6, drf[0, f : f + 1, :], drf[0, 16 + f : 17 + f, :]),
            two_rows(0, drf[1, f : f + 1, :], drf[1, 16 + f : 17 + f, :]),
            jnp.concatenate([third[0:56], north], axis=0),
        )
        q = sea * step(m * step(x, 0.2), 0.2)[8:56, 0:256]
        q_out[f] = q
        if f == 0:
            c00 = jnp.concatenate([coef[0:1, :], coef[0:1, :]], axis=1)
            heat = sea * (ss[0, 0] + c00 * q)
            for h in range(2):
                fs[pl.ds(h, 48, stride=2), :] = heat[:, 128 * h : 128 * h + 128]
            sst_s[...] = fs[0:96, :].astype(BF)
            for dl, dn in around:
                n = 40 + direction[(dl, dn)]
                back = 40 + direction[(-dl, -dn)]
                slot = (1 - dl) * 3 + 1 - dn
                send_to(lat_ok(dn), sst_s, sst_r.at[slot], n, back, lon_at(dl), lat + dn)
    sst_r[4] = sst_s[...]
    for dl, dn in around:
        arrive(lat_ok(dn), sst_r.at[(1 + dl) * 3 + 1 + dn], 40 + direction[(dl, dn)])
    sst_out[...] = sst_r[...]
    for finish in pending:
        finish()


def exchange(send, rows, cols, corn, atm, oce, mask, seam, mix_a, mix_o):
    return pl.pallas_call(
        middle_kernel,
        in_specs=[HERE] * 10,
        out_specs=[HERE] * 6,
        out_shape=[
            pltpu.VMEM((4, 16, 64, 256), F32),
            pltpu.VMEM((4, 16, 48, 256), F32),
            pltpu.VMEM((4, 48, 256), F32),
            pltpu.VMEM((8, 48, 256), F32),
            pltpu.VMEM((9, 96, 128), BF),
            pltpu.VMEM((16, 128), F32),
        ],
        scratch_shapes=[
            pltpu.VMEM((4, 16, 64, 256), F32),
            pltpu.VMEM((4, 32, 48, 256), F32),
            pltpu.VMEM((3, 8, 96, 128), BF),
            pltpu.VMEM((3, 8, 96, 128), BF),
            pltpu.VMEM((2, 8, 96, 128), BF),
            pltpu.VMEM((2, 8, 96, 128), BF),
            pltpu.VMEM((2, 2, 144, 256), BF),
            pltpu.VMEM((2, 160, 128), BF),
            pltpu.VMEM((4, 32, 128), BF),
            pltpu.VMEM((8, 2, 80, 256), BF),
            pltpu.VMEM((2, 2, 144, 256), F32),
            pltpu.VMEM((2, 80, 128), F32),
            pltpu.VMEM((2, 64, 128), F32),
            pltpu.VMEM((64, 384), F32),
            pltpu.VMEM((2048, 384), BF),
            pltpu.VMEM((2, 64, 128), F32),
            pltpu.VMEM((3, 48, 128), F32),
            pltpu.VMEM((2, 64, 256), F32),
            pltpu.VMEM((2, 2, 64, 256), F32),
            pltpu.VMEM((256, 256), BF),
            pltpu.VMEM((2, 256, 256), BF),
            pltpu.VMEM((2, 128, 256), BF),
            pltpu.VMEM((768, 128), F32),
            pltpu.VMEM((2, 32, 256), BF),
            pltpu.VMEM((2, 32, 256), BF),
            pltpu.VMEM((2, 48, 128), BF),
            pltpu.VMEM((2, 48, 128), BF),
            pltpu.VMEM((4, 16, 128), BF),
            pltpu.VMEM((8, 32, 256), BF),
            pltpu.VMEM((2, 32, 256), F32),
            pltpu.VMEM((2, 64, 128), F32),
            pltpu.VMEM((2, 16, 384), F32),
            pltpu.VMEM((96, 128), BF),
            pltpu.VMEM((9, 96, 128), BF),
            pltpu.SemaphoreType.DMA((1,)),
            pltpu.SemaphoreType.DMA((48,)),
            pltpu.SemaphoreType.DMA((48,)),
        ],
        compiler_params=pltpu.CompilerParams(collective_id=0, has_side_effects=True, vmem_limit_bytes=28 * MIB),
        name="exchange",
    )(send, rows, cols, corn, atm, oce, mask, seam, mix_a, mix_o)


def back_kernel(sst, dd, dt, q, coef, w, stepped, ss, flux, atm, ex, oce, f_out, sel, exs, exd, warm, sea, sem):
    plain = [
        pltpu.make_async_copy(flux, f_out, sem.at[0]),
        pltpu.make_async_copy(stepped.at[pl.ds(0, 2)], atm.at[pl.ds(0, 2)], sem.at[1]),
        pltpu.make_async_copy(stepped.at[2, pl.ds(0, 15)], atm.at[2, pl.ds(0, 15)], sem.at[2]),
        pltpu.make_async_copy(stepped.at[3], atm.at[3], sem.at[3]),
    ]
    for copy in plain:
        copy.start()
    heat = sst[...].reshape(864, 128)
    for k in range(3):
        picked = lax.dot_general(one_hot_slots(dd, dt, k), heat, TN, preferred_element_type=F32)
        sel[k * 128 : (k + 1) * 128, :] = picked.astype(BF)

    row = lax.broadcasted_iota(jnp.int32, (16, 128), 0)
    even = (row & 1) == 0
    ocean_out = lambda g: pltpu.make_async_copy(sea.at[pl.ds(g * 8, 8)], oce.at[pl.ds(g * 8, 8)], sem.at[6 + g])

    @pl.loop(0, 8)
    def _(g):
        v = g // 2
        for j in range(8):
            l = lax.rem(g, 2) * 8 + j
            c = coef[pl.ds(l, 1), :]
            sea[g * 8 + j] = ss[v, l] + jnp.concatenate([c, c], axis=1) * q[v]
        ocean_out(g).start()
        acc = jnp.zeros((16, 128), F32)
        t0 = pl.multiple_of(g * 16, 16)
        part = [sel[pl.ds(pl.multiple_of(k * 128 + t0, 16), 16), :] for k in range(3)]
        lhs = jnp.concatenate(part[:2], axis=1)
        last = part[2].astype(F32)
        split = jnp.concatenate([jnp.where(even, last, 0.0), jnp.where(even, 0.0, last)], axis=1).astype(BF)
        for j in range(0, 16, 4):
            quad = [[w[t0 + j + n, k] for k in range(3)] for n in range(4)]
            for h in range(2):
                p0, p1 = quad[2 * h], quad[2 * h + 1]
                block = jnp.concatenate([jnp.concatenate(p0[:2], axis=1), jnp.concatenate(p1[:2], axis=1)], axis=0)
                r = lax.dot_general(lhs, block, NT, preferred_element_type=F32)
                acc += jnp.where(row == j + 2 * h, r[:, :128], 0.0) + jnp.where(row == j + 2 * h + 1, r[:, 128:], 0.0)
            block = jnp.concatenate(
                [
                    jnp.concatenate([quad[0][2], quad[1][2]], axis=1),
                    jnp.concatenate([quad[2][2], quad[3][2]], axis=1),
                ],
                axis=0,
            )
            r = lax.dot_general(split, block, NT, preferred_element_type=F32)
            acc += jnp.where((row == j) | (row == j + 1), r[:, :128], 0.0)
            acc += jnp.where((row == j + 2) | (row == j + 3), r[:, 128:], 0.0)
        exs[pl.ds(t0, 16), :] = acc

    for h in range(2):
        at = slice(128 * h, 128 * h + 128)
        heat = exs[pl.ds(h, 64, stride=2), :]
        exd[:, at] = heat
        cold = stepped[2, 15, :, at]
        warm[:, at] = cold + 0.5 * (heat - cold)
    late = [
        pltpu.make_async_copy(exd, ex, sem.at[4]),
        pltpu.make_async_copy(warm, atm.at[2, 15], sem.at[5]),
    ]
    for copy in late:
        copy.start()
    for copy in plain + late:
        copy.wait()
    for g in range(8):
        ocean_out(g).wait()


def remap_back(sst, dd, dt, q, coef, w, stepped, ss, flux):
    return pl.pallas_call(
        back_kernel,
        in_specs=[HERE] * 9,
        out_specs=[AWAY] * 4,
        out_shape=[
            jax.ShapeDtypeStruct((4, 16, 64, 256), F32),
            jax.ShapeDtypeStruct((64, 256), F32),
            jax.ShapeDtypeStruct((64, 48, 256), F32),
            jax.ShapeDtypeStruct((8, 48, 256), F32),
        ],
        scratch_shapes=[
            pltpu.VMEM((384, 128), BF),
            pltpu.VMEM((128, 128), F32),
            pltpu.VMEM((64, 256), F32),
            pltpu.VMEM((64, 256), F32),
            pltpu.VMEM((64, 48, 256), F32),
            pltpu.SemaphoreType.DMA((14,)),
        ],
        compiler_params=pltpu.CompilerParams(vmem_limit_bytes=16 * MIB),
        name="remap_back",
    )(sst, dd, dt, q, coef, w, stepped, ss, flux)


def per_device(atmos, ts, sw, w, dd, dt, mix_a, ocean, mask, seam, mix_o):
    dd, dt = dd.T, dt.T
    send, rows, cols, corn, atm, oce, w = remap_out(atmos, ocean, ts, sw, w, dd, dt, mask)
    stepped, ss, q, flux, sst, coef = exchange(
        send, rows, cols, corn, atm, oce, mask, seam.reshape(1, 256), mix_a, mix_o
    )
    atm, ex, oce, flux = remap_back(sst, dd, dt, q, coef, w, stepped, ss, flux)
    return atm, ex, oce.reshape(ocean.shape), flux


def solution(mesh):
    field = P(None, None, "lat", "lon")
    plane = P("lat", "lon")
    tiles = P(("lon", "lat"), None)
    return jax.shard_map(
        per_device,
        mesh=mesh,
        in_specs=(field, plane, plane, P(("lon", "lat"), None, None, None), tiles, tiles, P(), field, plane, P("lon"), P()),
        out_specs=(field, plane, field, P(None, "lat", "lon")),
        check_vma=False,
    )
```

time: 111 us -> 67.9 us (0.61)
  Pallas kernels: 101 us -> 66.6 us
  local copies, waits for them, and re-layouts: 7.93 us -> 0.03 us
    pallas_call x3, Pallas kernels: 101 us -> 66.6 us  [the longest x1 49.6 us: exchange(): pl.pallas_call(middle_kernel, in_specs=[HERE] * 10, out_specs=[HERE] * 6,...]
    unnamed x24 -> x12, local copies, waits for them, and re-layouts: 7.93 us -> 0.03 us
where the time goes in v1:
time: 67.9 us; the launch traced here: 67.4 us
  Pallas kernels  66.6 us (98%)
  between operations  0.74 us (1%)
    pallas_call x1, Pallas kernels, exchange(): pl.pallas_call(middle_kernel, in_specs=[HERE] * 10, out_specs=[HERE] * 6,...  49.6 us
    pallas_call x1, Pallas kernels, remap_out(): pl.pallas_call(out_kernel, in_specs=[AWAY] * 8, out_specs=[HERE] * 7, out...  11.5 us
    pallas_call x1, Pallas kernels, remap_back(): pl.pallas_call(back_kernel, in_specs=[HERE] * 9, out_specs=[AWAY] * 4, ou...  5.52 us

profile of v1, /device:TPU:97, one launch (start us, length us, event | category | flops | bytes accessed | tf_op | source)
XLA Modules:
  0.0 67.4 jit_solution(16571801199706800662)
XLA Ops:
  0.6 0.0 copy-start
  0.6 0.0 copy-start.1
  0.7 0.0 copy-start.2
  0.7 0.0 copy-start.5
  0.7 11.5 %remap_out.1 = (bf16[9,8,96,128]{3,2,1,0:T(8,128)(2,1)S(1)}, bf16[4,144,256]{2,1,0:T(8,128)(2,1)S(1)}, bf16[2,160,128]{2,1,0:T(8,128)(2,1)S(1)}, bf16[4,32,128]{...) custom-call(f32[4,16,64,256]{3,2,1,0:T(8,128)} %atm.1, ...), custom_call_target="tpu_custom_call" | custom-call | tf_op jit(solution)/shard_map/remap_out/pallas_call | solution.py:178
  12.2 0.0 copy-done
  12.2 0.0 copy-done.1
  12.2 0.0 copy-done.2
  12.2 0.0 copy-done.5
  12.2 0.0 copy-start.3
  12.2 0.0 copy-start.4
  12.2 49.6 %exchange.1 = (f32[4,16,64,256]{3,2,1,0:T(8,128)S(1)}, f32[4,16,48,256]{3,2,1,0:T(8,128)S(1)}, f32[4,48,256]{2,1,0:T(8,128)S(1)}, f32[8,48,256]{2,1,0:T(8,128)S(...) custom-call(bf16[9,8,96,128]{3,2,1,0:T(8,128)(2,1)S(1)} %get-tuple-element.21.send, ...), custom_call_target="tpu_custom_call" | custom-call | tf_op jit(solution)/shard_map/exchange/pallas_call | solution.py:731
  61.8 0.0 copy-done.3
  61.8 0.0 copy-done.4
  61.8 5.5 %remap_back.1 = (f32[4,16,64,256]{3,2,1,0:T(8,128)}, f32[64,256]{1,0:T(8,128)}, f32[64,48,256]{2,1,0:T(8,128)}, f32[8,48,256]{2,1,0:T(8,128)}) custom-call(bf16[9,96,128]{2,1,0:T(8,128)(2,1)S(1)} %get-tuple-element.27.sst, s32[3,128]{1,0:T(4,128)S(1)} %bitcast.5, s32[3,128]{1,0:T(4,128)S(1)} %bitcast.7, f32[4,48,256]{2,1,0:T(8,128)S(1)} %get-tuple-element.28.q, ...), custom_call_target="tpu_custom_call" | custom-call | tf_op jit(solution)/shard_map/remap_back/pallas_call | solution.py:857
Async XLA Ops:
  0.6 11.5 %copy-start = (s32[48,256]{1,0:T(8,128)S(1)}, s32[48,256]{1,0:T(8,128)}, u32[]{:S(2)}) copy-start(s32[48,256]{1,0:T(8,128)} %mask.1) | copy-start | bytes 147460
  0.6 11.5 %copy-start.1 = (f32[16,16]{1,0:T(8,128)S(1)}, f32[16,16]{1,0:T(8,128)}, u32[]{:S(2)}) copy-start(f32[16,16]{1,0:T(8,128)} %mix_a.1) | copy-start | bytes 3076
  0.7 11.5 %copy-start.2 = (f32[16,16]{1,0:T(8,128)S(1)}, f32[16,16]{1,0:T(8,128)}, u32[]{:S(2)}) copy-start(f32[16,16]{1,0:T(8,128)} %mix_o.1) | copy-start | bytes 3076
  0.7 11.5 %copy-start.5 = (s32[256]{0:T(256)S(1)}, s32[256]{0:T(256)}, u32[]{:S(2)}) copy-start(s32[256]{0:T(256)} %param.20) | copy-start | bytes 3076
  12.2 49.6 %copy-start.3 = (s32[128,3]{0,1:T(4,128)S(1)}, s32[128,3]{0,1:T(4,128)}, u32[]{:S(2)}) copy-start(s32[128,3]{0,1:T(4,128)} %param.15) | copy-start | bytes 4612
  12.2 49.6 %copy-start.4 = (s32[128,3]{0,1:T(4,128)S(1)}, s32[128,3]{0,1:T(4,128)}, u32[]{:S(2)}) copy-start(s32[128,3]{0,1:T(4,128)} %param.16) | copy-start | bytes 4612

commit v2 on v1

--- a/solution.py
+++ b/solution.py
@@ -16,6 +16,8 @@
 N_LON = 8
 N_LAT = 16
 CHUNKS = 8
+EARLY = 4
+FIRST = 4
 MIB = 2**20
 
 
@@ -48,16 +50,173 @@
     return jnp.where(slot == rows, 1.0, 0.0).astype(BF)
 
 
-def out_kernel(
-    atm, oce, ts, sw, dd_far, dt_far, mask_far, w,
-    send, rows, cols, corn, atm_here, oce_here, w_here,
-    surf, heat, sun, dd, dt, mask, ft, terms, oh, tb, rbuf, sem,
+HERE = pl.BlockSpec(memory_space=pltpu.VMEM)
+AWAY = pl.BlockSpec(memory_space=pltpu.HBM)
+
+
+def step(x, rate):
+    rows, lanes = x.shape
+    around = pltpu.roll(x, 1, 0) + pltpu.roll(x, rows - 1, 0) + pltpu.roll(x, 1, 1) + pltpu.roll(x, lanes - 1, 1)
+    return (1.0 - 4.0 * rate) * x + rate * around
+
+
+def step_from(x, around, rate):
+    return (1.0 - 4.0 * rate) * x + rate * around
+
+
+def unpacked(from_left, from_right, n):
+    lane = lax.broadcasted_iota(jnp.int32, from_left.shape, 1)
+    right = pltpu.roll(from_right, (128 - 2 * n) & 127, 1)
+    left = pltpu.roll(from_left, 126 - 2 * n, 1)
+    return jnp.where(lane < 2, right, jnp.where(lane >= 126, left, 0.0))
+
+
+def two_rows(at, first, second):
+    rows = lax.broadcasted_iota(jnp.int32, (8, first.shape[1]), 0)
+    return jnp.where(rows == at, first, jnp.where(rows == at + 1, second, 0.0))
+
+
+def framed(x, south, north, third):
+    return jnp.concatenate([jnp.concatenate([south, x, north], axis=0), third], axis=1)
+
+
+def lateral(parts, tri):
+    rows = parts[0].shape[0]
+    total = jnp.dot(jnp.concatenate(parts, axis=0).astype(BF), tri, preferred_element_type=F32)
+    return [total[n * rows : (n + 1) * rows] for n in range(len(parts))]
+
+
+def near(x, inner, above, below, ghost):
+    rows = x.shape[0]
+    lane = lax.broadcasted_iota(jnp.int32, (rows, 128), 1)
+    row = lax.broadcasted_iota(jnp.int32, (8, 256), 0)
+    up = pltpu.roll(x, 1, 0)
+    down = pltpu.roll(x, rows - 1, 0)
+    up = jnp.concatenate([jnp.where(row == 0, above, up[0:8]), up[8:]], axis=0)
+    down = jnp.concatenate([down[: rows - 8], jnp.where(row == 7, below, down[rows - 8 :])], axis=0)
+    edges = jnp.concatenate([jnp.where(lane == 0, ghost, 0.0), jnp.where(lane == 127, ghost, 0.0)], axis=1)
+    return up + down + inner + edges
+
+
+def beside(x, ghost, lane):
+    t0, t1 = x[:, 0:128], x[:, 128:256]
+    r0, r1 = pltpu.roll(t0, 1, 1), pltpu.roll(t1, 1, 1)
+    l0, l1 = pltpu.roll(t0, 127, 1), pltpu.roll(t1, 127, 1)
+    first, last = lane == 0, lane == 127
+    s0 = jnp.where(first, ghost, r0) + jnp.where(last, l1, l0)
+    s1 = jnp.where(first, r0, r1) + jnp.where(last, ghost, l1)
+    return jnp.concatenate([s0, s1], axis=1)
+
+
+def beside_packed(left, right, own_left, own_right, odd):
+    centre = jnp.where(odd, left, right)
+    outer = jnp.where(odd, pltpu.roll(left, 1, 1), pltpu.roll(right, 127, 1))
+    inner = jnp.where(odd, pltpu.roll(own_left, 1, 1), pltpu.roll(own_right, 127, 1))
+    return centre, outer + inner
+
+
+def corner_lanes(centre, row):
+    lane = lax.broadcasted_iota(jnp.int32, (64, 128), 1)
+    field = lax.broadcasted_iota(jnp.int32, (64, 128), 0)
+    line = jnp.broadcast_to(centre[row : row + 1, :], (64, 128))
+    left = jnp.sum(jnp.where(lane == 2 * field + 1, line, 0.0), axis=1, keepdims=True)
+    right = jnp.sum(jnp.where(lane == 2 * field, line, 0.0), axis=1, keepdims=True)
+    return jnp.where(lane == 0, left, jnp.where(lane == 127, right, 0.0))
+
+
+def spread(mixer, cells):
+    size = 16 * cells
+    pick = lambda dim: jnp.where(
+        lax.broadcasted_iota(jnp.int32, (size, 16) if dim == 0 else (16, size), dim) // cells
+        == lax.broadcasted_iota(jnp.int32, (size, 16) if dim == 0 else (16, size), 1 - dim),
+        1.0,
+        0.0,
+    )
+    dot = functools.partial(jnp.dot, precision=HIGHEST, preferred_element_type=F32)
+    full = dot(dot(pick(0), mixer), pick(1))
+    r = lax.broadcasted_iota(jnp.int32, (size, size), 0) % cells
+    c = lax.broadcasted_iota(jnp.int32, (size, size), 1) % cells
+    return jnp.where(r == c, full, 0.0)
+
+
+def halves(x):
+    high = x.astype(BF)
+    return high, (x - high.astype(F32)).astype(BF)
+
+
+def dot3(lhs_high, lhs_low, x):
+    high, low = halves(x)
+    dot = functools.partial(jnp.dot, preferred_element_type=F32)
+    return dot(lhs_high, high) + dot(lhs_high, low) + dot(lhs_low, high)
+
+
+def exchange_kernel(
+    atm_far, oce_far, ts_far, sw_far, dd_far, dt_far, mask_far, w_far, seam, mix_a, mix_o,
+    w_here, stepped, ss, q_out, f_out, sst_out, coef_out,
+    atm, oce, surf, heat, sun, dd, dt, mask, ft, terms, oh, tb, rbuf, rows, cols, corn, send,
+    bc, pr, ro, rl, sl, rr, cc, kk, fr, rrf, cea, ceo, mext, fold, gsa, gso, gea, geo, tri,
+    ka, ko, fs, dr_s, dr_r, dc_s, dc_r, dk_r, fd, drf, ced, gd, sst_s, sst_r,
+    sem, lsem, ssem, rsem,
 ):
+    lon = lax.axis_index("lon")
+    lat = lax.axis_index("lat")
+    side = lax.rem(lat, 2)
+    partner = lat + 1 - 2 * side
+    outer = lat - 1 + 2 * side
+    has_outer = jnp.logical_and(outer >= 0, outer < N_LAT)
+    has_south = lat > 0
+    has_north = lat < N_LAT - 1
+    top = lat == N_LAT - 1
+    always = lat >= 0
+    lon_at = lambda d: lax.rem(lon + d + N_LON, N_LON)
+
+    def lat_ok(d):
+        return always if d == 0 else (has_south if d < 0 else has_north)
+
+    def send_to(cond, src, dst, n, m, dev_lon, dev_lat):
+        copy = pltpu.make_async_remote_copy(
+            src_ref=src, dst_ref=dst, send_sem=ssem.at[n], recv_sem=rsem.at[m],
+            device_id=(dev_lon, dev_lat), device_id_type=MESH,
+        )
+
+        @pl.when(cond)
+        def _():
+            copy.start()
+
+        def finish():
+            @pl.when(cond)
+            def _():
+                copy.wait_send()
+
+        pending.append(finish)
+
+    def arrive(cond, dst, m):
+        @pl.when(cond)
+        def _():
+            pltpu.make_async_remote_copy(
+                src_ref=dst, dst_ref=dst, send_sem=ssem.at[0], recv_sem=rsem.at[m],
+                device_id=(lon, partner), device_id_type=MESH,
+            ).wait_recv()
+
+    pending = []
+    barrier = pltpu.get_barrier_semaphore()
+    around = [(dl, dn) for dl in (-1, 0, 1) for dn in (-1, 0, 1) if (dl, dn) != (0, 0)]
+    for dl, dn in around:
+
+        @pl.when(lat_ok(dn))
+        def _(dl=dl, dn=dn):
+            pl.semaphore_signal(barrier, inc=1, device_id=(lon_at(dl), lat + dn), device_id_type=MESH)
+
+    @pl.when(top)
+    def _():
+        for d in range(2, N_LON - 1):
+            pl.semaphore_signal(barrier, inc=1, device_id=(lon_at(d), lat), device_id_type=MESH)
+
     chunk = 128 // CHUNKS
     copies = [
-        pltpu.make_async_copy(atm.at[:, 15], surf, sem.at[0]),
-        pltpu.make_async_copy(ts, heat, sem.at[1]),
-        pltpu.make_async_copy(sw, sun, sem.at[2]),
+        pltpu.make_async_copy(atm_far.at[:, 15], surf, sem.at[0]),
+        pltpu.make_async_copy(ts_far, heat, sem.at[1]),
+        pltpu.make_async_copy(sw_far, sun, sem.at[2]),
         pltpu.make_async_copy(mask_far, mask, sem.at[5 + CHUNKS]),
     ]
     targets = [
@@ -67,18 +226,20 @@
     for copy in targets:
         copy.start()
     weights = lambda i: pltpu.make_async_copy(
-        w.at[pl.ds(i * chunk, chunk)], w_here.at[pl.ds(i * chunk, chunk)], sem.at[3 + i]
+        w_far.at[pl.ds(i * chunk, chunk)], w_here.at[pl.ds(i * chunk, chunk)], sem.at[3 + i]
     )
     fields = [
-        pltpu.make_async_copy(atm, atm_here, sem.at[3 + CHUNKS]),
-        pltpu.make_async_copy(oce, oce_here, sem.at[4 + CHUNKS]),
+        pltpu.make_async_copy(atm_far, atm, sem.at[3 + CHUNKS]),
+        pltpu.make_async_copy(oce_far, oce, sem.at[4 + CHUNKS]),
     ]
     for copy in copies:
         copy.start()
-    for i in range(CHUNKS):
+    for i in range(EARLY):
         weights(i).start()
     for copy in fields:
         copy.start()
+    for i in range(EARLY, CHUNKS):
+        weights(i).start()
 
     for copy in targets:
         copy.wait()
@@ -94,8 +255,7 @@
     group = lax.broadcasted_iota(jnp.int32, (32, 128), 0)
     even = (group & 8) == 0
 
-    @pl.loop(0, CHUNKS)
-    def _(i):
+    def remap_chunk(i):
         weights(i).wait()
         for j in range(0, chunk, 4):
             t = i * chunk + j
@@ -120,6 +280,10 @@
             terms[pl.ds(at, 16), :] = r[:16, :128]
             terms[pl.ds(at + 16, 16), :] = r[16:, 128:]
 
+    @pl.loop(0, EARLY)
+    def _(i):
+        remap_chunk(i)
+
     for copy in fields:
         copy.wait()
     lane_a = lax.broadcasted_iota(jnp.int32, (64, 128), 1) >> 1
@@ -134,235 +298,35 @@
             n = v * 16 + l
             ahead = 2 * n
             back = (2 * n + 2) & 127
-            left_a = jnp.where(lane_a == n, pltpu.roll(atm_here[v, l, :, 0:128], ahead, 1), left_a)
-            right_a = jnp.where(lane_a == n, pltpu.roll(atm_here[v, l, :, 128:256], back, 1), right_a)
-            left_o = jnp.where(lane_o == n, pltpu.roll(oce_here[v, l, :, 0:128], ahead, 1), left_o)
-            right_o = jnp.where(lane_o == n, pltpu.roll(oce_here[v, l, :, 128:256], back, 1), right_o)
+            left_a = jnp.where(lane_a == n, pltpu.roll(atm[v, l, :, 0:128], ahead, 1), left_a)
+            right_a = jnp.where(lane_a == n, pltpu.roll(atm[v, l, :, 128:256], back, 1), right_a)
+            left_o = jnp.where(lane_o == n, pltpu.roll(oce[v, l, :, 0:128], ahead, 1), left_o)
+            right_o = jnp.where(lane_o == n, pltpu.roll(oce[v, l, :, 128:256], back, 1), right_o)
             for e in range(2):
-                rbuf[e, pl.ds(n, 1), :] = atm_here[v, l, e : e + 1, :]
-                rbuf[2 + e, pl.ds(n, 1), :] = atm_here[v, l, 62 + e : 63 + e, :]
-                rbuf[e, pl.ds(64 + n, 1), :] = oce_here[v, l, e : e + 1, :]
-                rbuf[2 + e, pl.ds(64 + n, 1), :] = oce_here[v, l, 46 + e : 47 + e, :]
+                rbuf[e, pl.ds(n, 1), :] = atm[v, l, e : e + 1, :]
+                rbuf[2 + e, pl.ds(n, 1), :] = atm[v, l, 62 + e : 63 + e, :]
+                rbuf[e, pl.ds(64 + n, 1), :] = oce[v, l, e : e + 1, :]
+                rbuf[2 + e, pl.ds(64 + n, 1), :] = oce[v, l, 46 + e : 47 + e, :]
         return left_a, right_a, left_o, right_o
 
     sea = mask[...].astype(F32)
-    for side in range(2):
-        cols_a, cols_o = packed[side], packed[2 + side]
-        cols[side, 0:64, :] = cols_a.astype(BF)
-        cols[side, 64:112, :] = cols_o.astype(BF)
-        cols[side, 112:160, :] = sea[:, 128 * side : 128 * side + 128].astype(BF)
-        corn[2 * side, 0:16, :] = cols_a[0:16].astype(BF)
-        corn[2 * side, 16:32, :] = cols_o[0:16].astype(BF)
-        corn[2 * side + 1, 0:16, :] = cols_a[48:64].astype(BF)
-        corn[2 * side + 1, 16:32, :] = cols_o[32:48].astype(BF)
+    for a in range(2):
+        cols_a, cols_o = packed[a], packed[2 + a]
+        cols[a, 0:64, :] = cols_a.astype(BF)
+        cols[a, 64:112, :] = cols_o.astype(BF)
+        cols[a, 112:160, :] = sea[:, 128 * a : 128 * a + 128].astype(BF)
+        corn[2 * a, 0:16, :] = cols_a[0:16].astype(BF)
+        corn[2 * a, 16:32, :] = cols_o[0:16].astype(BF)
+        corn[2 * a + 1, 0:16, :] = cols_a[48:64].astype(BF)
+        corn[2 * a + 1, 16:32, :] = cols_o[32:48].astype(BF)
     for e in range(2):
         for b in range(2):
             r = 46 * b + e
             rbuf[2 * b + e, 128:144, :] = jnp.broadcast_to(sea[r : r + 1, :], (16, 256))
     rows[...] = rbuf[...].astype(BF)
 
-    for f in range(8):
-        tb[:, f * 128 : (f + 1) * 128] = terms[pl.ds(f, 384, stride=8), :].astype(BF)
-    for g in range(4):
-        res = jnp.dot(oh[...], tb[:, g * 256 : (g + 1) * 256], preferred_element_type=F32)
-        for o in range(9):
-            for b in range(2):
-                send[o, 2 * g + b] = res[o * 96 : (o + 1) * 96, b * 128 : (b + 1) * 128].astype(BF)
-
-
-HERE = pl.BlockSpec(memory_space=pltpu.VMEM)
-AWAY = pl.BlockSpec(memory_space=pltpu.HBM)
-
-
-def remap_out(atm, oce, ts, sw, w, dd, dt, mask):
-    return pl.pallas_call(
-        out_kernel,
-        in_specs=[AWAY] * 8,
-        out_specs=[HERE] * 7,
-        out_shape=[
-            pltpu.VMEM((9, 8, 96, 128), BF),
-            pltpu.VMEM((4, 144, 256), BF),
-            pltpu.VMEM((2, 160, 128), BF),
-            pltpu.VMEM((4, 32, 128), BF),
-            pltpu.VMEM((4, 16, 64, 256), F32),
-            pltpu.VMEM((4, 16, 48, 256), F32),
-            pltpu.VMEM((128, 3, 128, 128), BF),
-        ],
-        scratch_shapes=[
-            pltpu.VMEM((4, 64, 256), F32),
-            pltpu.VMEM((64, 256), F32),
-            pltpu.VMEM((64, 256), F32),
-            pltpu.VMEM((3, 128), jnp.int32),
-            pltpu.VMEM((3, 128), jnp.int32),
-            pltpu.VMEM((48, 256), jnp.int32),
-            pltpu.VMEM((1024, 128), F32),
-            pltpu.VMEM((3072, 128), F32),
-            pltpu.VMEM((864, 384), BF),
-            pltpu.VMEM((384, 1024), BF),
-            pltpu.VMEM((4, 144, 256), F32),
-            pltpu.SemaphoreType.DMA((8 + CHUNKS,)),
-        ],
-        compiler_params=pltpu.CompilerParams(vmem_limit_bytes=16 * MIB),
-        name="remap_out",
-    )(*[pltpu.with_memory_space_constraint(x, pltpu.HBM) for x in (atm, oce, ts, sw, dd, dt, mask, w)])
-
-
-def step(x, rate):
-    rows, lanes = x.shape
-    around = pltpu.roll(x, 1, 0) + pltpu.roll(x, rows - 1, 0) + pltpu.roll(x, 1, 1) + pltpu.roll(x, lanes - 1, 1)
-    return (1.0 - 4.0 * rate) * x + rate * around
-
-
-def step_from(x, around, rate):
-    return (1.0 - 4.0 * rate) * x + rate * around
-
-
-def unpacked(from_left, from_right, n):
-    lane = lax.broadcasted_iota(jnp.int32, from_left.shape, 1)
-    right = pltpu.roll(from_right, (128 - 2 * n) & 127, 1)
-    left = pltpu.roll(from_left, 126 - 2 * n, 1)
-    return jnp.where(lane < 2, right, jnp.where(lane >= 126, left, 0.0))
-
-
-def two_rows(at, first, second):
-    rows = lax.broadcasted_iota(jnp.int32, (8, first.shape[1]), 0)
-    return jnp.where(rows == at, first, jnp.where(rows == at + 1, second, 0.0))
-
-
-def framed(x, south, north, third):
-    return jnp.concatenate([jnp.concatenate([south, x, north], axis=0), third], axis=1)
-
-
-def lateral(parts, tri):
-    rows = parts[0].shape[0]
-    total = jnp.dot(jnp.concatenate(parts, axis=0).astype(BF), tri, preferred_element_type=F32)
-    return [total[n * rows : (n + 1) * rows] for n in range(len(parts))]
-
-
-def near(x, inner, above, below, ghost):
-    rows = x.shape[0]
-    lane = lax.broadcasted_iota(jnp.int32, (rows, 128), 1)
-    row = lax.broadcasted_iota(jnp.int32, (8, 256), 0)
-    up = pltpu.roll(x, 1, 0)
-    down = pltpu.roll(x, rows - 1, 0)
-    up = jnp.concatenate([jnp.where(row == 0, above, up[0:8]), up[8:]], axis=0)
-    down = jnp.concatenate([down[: rows - 8], jnp.where(row == 7, below, down[rows - 8 :])], axis=0)
-    edges = jnp.concatenate([jnp.where(lane == 0, ghost, 0.0), jnp.where(lane == 127, ghost, 0.0)], axis=1)
-    return up + down + inner + edges
-
-
-def beside(x, ghost, lane):
-    t0, t1 = x[:, 0:128], x[:, 128:256]
-    r0, r1 = pltpu.roll(t0, 1, 1), pltpu.roll(t1, 1, 1)
-    l0, l1 = pltpu.roll(t0, 127, 1), pltpu.roll(t1, 127, 1)
-    first, last = lane == 0, lane == 127
-    s0 = jnp.where(first, ghost, r0) + jnp.where(last, l1, l0)
-    s1 = jnp.where(first, r0, r1) + jnp.where(last, ghost, l1)
-    return jnp.concatenate([s0, s1], axis=1)
-
-
-def beside_packed(left, right, own_left, own_right, odd):
-    centre = jnp.where(odd, left, right)
-    outer = jnp.where(odd, pltpu.roll(left, 1, 1), pltpu.roll(right, 127, 1))
-    inner = jnp.where(odd, pltpu.roll(own_left, 1, 1), pltpu.roll(own_right, 127, 1))
-    return centre, outer + inner
-
-
-def corner_lanes(centre, row):
-    lane = lax.broadcasted_iota(jnp.int32, (64, 128), 1)
-    field = lax.broadcasted_iota(jnp.int32, (64, 128), 0)
-    line = jnp.broadcast_to(centre[row : row + 1, :], (64, 128))
-    left = jnp.sum(jnp.where(lane == 2 * field + 1, line, 0.0), axis=1, keepdims=True)
-    right = jnp.sum(jnp.where(lane == 2 * field, line, 0.0), axis=1, keepdims=True)
-    return jnp.where(lane == 0, left, jnp.where(lane == 127, right, 0.0))
-
-
-def spread(mixer, cells):
-    size = 16 * cells
-    pick = lambda dim: jnp.where(
-        lax.broadcasted_iota(jnp.int32, (size, 16) if dim == 0 else (16, size), dim) // cells
-        == lax.broadcasted_iota(jnp.int32, (size, 16) if dim == 0 else (16, size), 1 - dim),
-        1.0,
-        0.0,
-    )
-    dot = functools.partial(jnp.dot, precision=HIGHEST, preferred_element_type=F32)
-    full = dot(dot(pick(0), mixer), pick(1))
-    r = lax.broadcasted_iota(jnp.int32, (size, size), 0) % cells
-    c = lax.broadcasted_iota(jnp.int32, (size, size), 1) % cells
-    return jnp.where(r == c, full, 0.0)
-
-
-def halves(x):
-    high = x.astype(BF)
-    return high, (x - high.astype(F32)).astype(BF)
-
-
-def dot3(lhs_high, lhs_low, x):
-    high, low = halves(x)
-    dot = functools.partial(jnp.dot, preferred_element_type=F32)
-    return dot(lhs_high, high) + dot(lhs_high, low) + dot(lhs_low, high)
-
-
-def middle_kernel(
-    send, rows, cols, corn, atm, oce, mask, seam, mix_a, mix_o,
-    stepped, ss, q_out, f_out, sst_out, coef_out,
-    lla, bc, pr, ro, rl, sl, rr, cc, kk, fr, rrf, cea, ceo, mext, fold, gsa, gso, gea, geo, tri,
-    ka, ko, fs, dr_s, dr_r, dc_s, dc_r, dk_r, fd, drf, ced, gd, sst_s, sst_r,
-    lsem, ssem, rsem,
-):
-    lon = lax.axis_index("lon")
-    lat = lax.axis_index("lat")
-    side = lax.rem(lat, 2)
-    partner = lat + 1 - 2 * side
-    outer = lat - 1 + 2 * side
-    has_outer = jnp.logical_and(outer >= 0, outer < N_LAT)
-    has_south = lat > 0
-    has_north = lat < N_LAT - 1
-    top = lat == N_LAT - 1
-    always = lat >= 0
-    lon_at = lambda d: lax.rem(lon + d + N_LON, N_LON)
-
-    def lat_ok(d):
-        return always if d == 0 else (has_south if d < 0 else has_north)
-
-    def send_to(cond, src, dst, n, m, dev_lon, dev_lat):
-        copy = pltpu.make_async_remote_copy(
-            src_ref=src, dst_ref=dst, send_sem=ssem.at[n], recv_sem=rsem.at[m],
-            device_id=(dev_lon, dev_lat), device_id_type=MESH,
-        )
-
-        @pl.when(cond)
-        def _():
-            copy.start()
-
-        def finish():
-            @pl.when(cond)
-            def _():
-                copy.wait_send()
-
-        pending.append(finish)
-
-    def arrive(cond, dst, m):
-        @pl.when(cond)
-        def _():
-            pltpu.make_async_remote_copy(
-                src_ref=dst, dst_ref=dst, send_sem=ssem.at[0], recv_sem=rsem.at[m],
-                device_id=(lon, partner), device_id_type=MESH,
-            ).wait_recv()
-
-    pending = []
-    barrier = pltpu.get_barrier_semaphore()
-    around = [(dl, dn) for dl in (-1, 0, 1) for dn in (-1, 0, 1) if (dl, dn) != (0, 0)]
-    for dl, dn in around:
-
-        @pl.when(lat_ok(dn))
-        def _(dl=dl, dn=dn):
-            pl.semaphore_signal(barrier, inc=1, device_id=(lon_at(dl), lat + dn), device_id_type=MESH)
-
     @pl.when(top)
     def _():
-        for d in range(2, N_LON - 1):
-            pl.semaphore_signal(barrier, inc=1, device_id=(lon_at(d), lat), device_id_type=MESH)
         pl.semaphore_wait(barrier, 5 + 5)
 
     @pl.when(lat == 0)
@@ -418,6 +382,19 @@
     def _():
         own_fold.start()
 
+    @pl.loop(EARLY, CHUNKS)
+    def _(i):
+        remap_chunk(i)
+
+    for f in range(8):
+        tb[:, f * 128 : (f + 1) * 128] = terms[pl.ds(f, 384, stride=8), :].astype(BF)
+    for g in range(4):
+        res = jnp.dot(oh[...], tb[:, g * 256 : (g + 1) * 256], preferred_element_type=F32)
+        for o in range(9):
+            for b in range(2):
+                send[o, 2 * g + b] = res[o * 96 : (o + 1) * 96, b * 128 : (b + 1) * 128].astype(BF)
+
+
     for dl in (0, 2, 1):
         send_to(always, send.at[dl * 3 + 2 - 2 * side], pr.at[dl], 16 + dl, 16 + dl, lon, partner)
     for dl in range(3):
@@ -438,16 +415,6 @@
                 dk_r[2 * a + b] = jnp.zeros(dk_r.shape[1:], BF)
             for dl in range(3):
                 sst_r[dl * 3 + 2 * b] = jnp.zeros(sst_r.shape[1:], BF)
-
-    for dl in (0, 2, 1):
-        arrive(always, pr.at[dl], 16 + dl)
-    for n, dl in enumerate((0, 2)):
-
-        @pl.loop(0, 8)
-        def _(f, n=n, dl=dl):
-            sl[n, f] = (send[3 * dl + 1, f].astype(F32) + pr[dl, f].astype(F32)).astype(BF)
-
-        send_to(always, sl.at[n], rl.at[n], 22 + n, 22 + n, lon_at(dl - 1), lat)
 
     ma = mix_a[...]
     mo = mix_o[...]
@@ -566,6 +533,16 @@
     c256 = lax.broadcasted_iota(jnp.int32, (256, 256), 1)
     tri[...] = jnp.where(jnp.logical_or(r256 == c256 + 1, r256 + 1 == c256), 1.0, 0.0).astype(BF)
 
+    for dl in (0, 2, 1):
+        arrive(always, pr.at[dl], 16 + dl)
+    for n, dl in enumerate((0, 2)):
+
+        @pl.loop(0, 8)
+        def _(f, n=n, dl=dl):
+            sl[n, f] = (send[3 * dl + 1, f].astype(F32) + pr[dl, f].astype(F32)).astype(BF)
+
+        send_to(always, sl.at[n], rl.at[n], 22 + n, 22 + n, lon_at(dl - 1), lat)
+
     @pl.loop(0, 8)
     def _(i):
         v = i // 2
@@ -597,8 +574,7 @@
         wet = mask[pl.ds(at, 8), :] > 0
         ss[v, :, pl.ds(at, 8), :] = jnp.where(wet[None], mixed, oce[v, :, pl.ds(at, 8), :])
 
-    @pl.loop(0, 8)
-    def _(i):
+    def atm_group(i):
         v = i // 2
         first = pl.multiple_of(lax.rem(i, 2) * 8, 8)
         lines = pl.ds(pl.multiple_of(i * 8, 8), 8)
@@ -613,14 +589,11 @@
                 for j, x in enumerate(parts)
             ]
         for j, y in enumerate(parts):
-            lla[v, first + j] = y
-
-    @pl.loop(0, 16, unroll=4)
-    def _(n):
-        v = n // 4
-        at = pl.multiple_of(lax.rem(n, 4) * 16, 16)
-        mixed = dot3(ka[0], ka[1], lla[v, :, pl.ds(at, 16), :].reshape(256, 256))
-        stepped[v, :, pl.ds(at, 16), :] = mixed.reshape(16, 16, 256)
+            stepped[v, first + j] = y
+
+    @pl.loop(0, FIRST)
+    def _(i):
+        atm_group(i)
 
     for dl in range(3):
         arrive(has_outer, ro.at[dl], 19 + dl)
@@ -671,6 +644,10 @@
     @pl.when(top)
     def _():
         fd[lon] = dr_s[1]
+
+    @pl.loop(FIRST, 8)
+    def _(i):
+        atm_group(i)
 
     halo_arrive(24, rows_r, cols_r, corn_r)
     for b in range(2):
@@ -719,6 +696,13 @@
                 back = 40 + direction[(-dl, -dn)]
                 slot = (1 - dl) * 3 + 1 - dn
                 send_to(lat_ok(dn), sst_s, sst_r.at[slot], n, back, lon_at(dl), lat + dn)
+    @pl.loop(0, 16, unroll=4)
+    def _(n):
+        v = n // 4
+        at = pl.multiple_of(lax.rem(n, 4) * 16, 16)
+        mixed = dot3(ka[0], ka[1], stepped[v, :, pl.ds(at, 16), :].reshape(256, 256))
+        stepped[v, :, pl.ds(at, 16), :] = mixed.reshape(16, 16, 256)
+
     sst_r[4] = sst_s[...]
     for dl, dn in around:
         arrive(lat_ok(dn), sst_r.at[(1 + dl) * 3 + 1 + dn], 40 + direction[(dl, dn)])
@@ -727,12 +711,14 @@
         finish()
 
 
-def exchange(send, rows, cols, corn, atm, oce, mask, seam, mix_a, mix_o):
+def exchange(atm, oce, ts, sw, w, dd, dt, mask, seam, mix_a, mix_o):
+    far = [pltpu.with_memory_space_constraint(x, pltpu.HBM) for x in (atm, oce, ts, sw, dd, dt, mask, w)]
     return pl.pallas_call(
-        middle_kernel,
-        in_specs=[HERE] * 10,
-        out_specs=[HERE] * 6,
+        exchange_kernel,
+        in_specs=[AWAY] * 8 + [HERE] * 3,
+        out_specs=[HERE] * 7,
         out_shape=[
+            pltpu.VMEM((128, 3, 128, 128), BF),
             pltpu.VMEM((4, 16, 64, 256), F32),
             pltpu.VMEM((4, 16, 48, 256), F32),
             pltpu.VMEM((4, 48, 256), F32),
@@ -742,6 +728,22 @@
         ],
         scratch_shapes=[
             pltpu.VMEM((4, 16, 64, 256), F32),
+            pltpu.VMEM((4, 16, 48, 256), F32),
+            pltpu.VMEM((4, 64, 256), F32),
+            pltpu.VMEM((64, 256), F32),
+            pltpu.VMEM((64, 256), F32),
+            pltpu.VMEM((3, 128), jnp.int32),
+            pltpu.VMEM((3, 128), jnp.int32),
+            pltpu.VMEM((48, 256), jnp.int32),
+            pltpu.VMEM((1024, 128), F32),
+            pltpu.VMEM((3072, 128), F32),
+            pltpu.VMEM((864, 384), BF),
+            pltpu.VMEM((384, 1024), BF),
+            pltpu.VMEM((4, 144, 256), F32),
+            pltpu.VMEM((4, 144, 256), BF),
+            pltpu.VMEM((2, 160, 128), BF),
+            pltpu.VMEM((4, 32, 128), BF),
+            pltpu.VMEM((9, 8, 96, 128), BF),
             pltpu.VMEM((4, 32, 48, 256), F32),
             pltpu.VMEM((3, 8, 96, 128), BF),
             pltpu.VMEM((3, 8, 96, 128), BF),
@@ -775,13 +777,14 @@
             pltpu.VMEM((2, 16, 384), F32),
             pltpu.VMEM((96, 128), BF),
             pltpu.VMEM((9, 96, 128), BF),
+            pltpu.SemaphoreType.DMA((8 + CHUNKS,)),
             pltpu.SemaphoreType.DMA((1,)),
             pltpu.SemaphoreType.DMA((48,)),
             pltpu.SemaphoreType.DMA((48,)),
         ],
-        compiler_params=pltpu.CompilerParams(collective_id=0, has_side_effects=True, vmem_limit_bytes=28 * MIB),
+        compiler_params=pltpu.CompilerParams(collective_id=0, has_side_effects=True, vmem_limit_bytes=36 * MIB),
         name="exchange",
-    )(send, rows, cols, corn, atm, oce, mask, seam, mix_a, mix_o)
+    )(*far, seam, mix_a, mix_o)
 
 
 def back_kernel(sst, dd, dt, q, coef, w, stepped, ss, flux, atm, ex, oce, f_out, sel, exs, exd, warm, sea, sem):
@@ -879,9 +882,8 @@
 
 def per_device(atmos, ts, sw, w, dd, dt, mix_a, ocean, mask, seam, mix_o):
     dd, dt = dd.T, dt.T
-    send, rows, cols, corn, atm, oce, w = remap_out(atmos, ocean, ts, sw, w, dd, dt, mask)
-    stepped, ss, q, flux, sst, coef = exchange(
-        send, rows, cols, corn, atm, oce, mask, seam.reshape(1, 256), mix_a, mix_o
+    w, stepped, ss, q, flux, sst, coef = exchange(
+        atmos, ocean, ts, sw, w, dd, dt, mask, seam.reshape(1, 256), mix_a, mix_o
     )
     atm, ex, oce, flux = remap_back(sst, dd, dt, q, coef, w, stepped, ss, flux)
     return atm, ex, oce.reshape(ocean.shape), flux

time: 67.9 us -> 55.1 us (0.81)
  Pallas kernels: 66.6 us -> 53.6 us
    pallas_call x2 -> x1, Pallas kernels: 61.1 us -> 48.1 us  [exchange(): pl.pallas_call(exchange_kernel, in_specs=[AWAY] * 8 + [HERE] * 3, out_spe...]
where the time goes in v2:
time: 55.1 us; the launch traced here: 54.3 us
  Pallas kernels  53.6 us (97%)
  between operations  0.67 us (1%)
    pallas_call x1, Pallas kernels, exchange(): pl.pallas_call(exchange_kernel, in_specs=[AWAY] * 8 + [HERE] * 3, out_spe...  48.1 us
    pallas_call x1, Pallas kernels, remap_back(): pl.pallas_call(back_kernel, in_specs=[HERE] * 9, out_specs=[AWAY] * 4, ou...  5.51 us

profile of v2, /device:TPU:97, one launch (start us, length us, event | category | flops | bytes accessed | tf_op | source)
XLA Modules:
  0.0 54.3 jit_solution(15894729867141495837)
XLA Ops:
  0.6 0.0 copy-start
  0.6 0.0 copy-start.1
  0.7 48.1 %exchange.1 = (bf16[128,3,128,128]{3,2,1,0:T(8,128)(2,1)S(1)}, f32[4,16,64,256]{3,2,1,0:T(8,128)S(1)}, f32[4,16,48,256]{3,2,1,0:T(8,128)S(1)}, f32[4,48,256]{2,1...) custom-call(f32[4,16,64,256]{3,2,1,0:T(8,128)} %atm_far.1, ...), custom_call_target="tpu_custom_call" | custom-call | tf_op jit(solution)/shard_map/exchange/pallas_call | solution.py:716
  48.8 0.0 copy-done
  48.8 0.0 copy-done.1
  48.8 5.5 %remap_back.1 = (f32[4,16,64,256]{3,2,1,0:T(8,128)}, f32[64,256]{1,0:T(8,128)}, f32[64,48,256]{2,1,0:T(8,128)}, f32[8,48,256]{2,1,0:T(8,128)}) custom-call(bf16[9,96,128]{2,1,0:T(8,128)(2,1)S(1)} %get-tuple-element.15.sst, s32[3,128]{1,0:T(4,128)S(1)} %bitcast.5, s32[3,128]{1,0:T(4,128)S(1)} %bitcast.7, f32[4,48,256]{2,1,0:T(8,128)S(1)} %get-tuple-element.16.q, ...), custom_call_target="tpu_custom_call" | custom-call | tf_op jit(solution)/shard_map/remap_back/pallas_call | solution.py:860
Async XLA Ops:
  0.6 48.1 %copy-start = (s32[128,3]{0,1:T(4,128)S(1)}, s32[128,3]{0,1:T(4,128)}, u32[]{:S(2)}) copy-start(s32[128,3]{0,1:T(4,128)} %param.15) | copy-start | bytes 4612
  0.6 48.1 %copy-start.1 = (s32[128,3]{0,1:T(4,128)S(1)}, s32[128,3]{0,1:T(4,128)}, u32[]{:S(2)}) copy-start(s32[128,3]{0,1:T(4,128)} %param.16) | copy-start | bytes 4612

commit v3 on v2

--- a/solution.py
+++ b/solution.py
@@ -16,8 +16,9 @@
 N_LON = 8
 N_LAT = 16
 CHUNKS = 8
-EARLY = 4
 FIRST = 4
+MIXED = 8
+DETOUR = 2
 MIB = 2**20
 
 
@@ -154,7 +155,7 @@
     atm_far, oce_far, ts_far, sw_far, dd_far, dt_far, mask_far, w_far, seam, mix_a, mix_o,
     w_here, stepped, ss, q_out, f_out, sst_out, coef_out,
     atm, oce, surf, heat, sun, dd, dt, mask, ft, terms, oh, tb, rbuf, rows, cols, corn, send,
-    bc, pr, ro, rl, sl, rr, cc, kk, fr, rrf, cea, ceo, mext, fold, gsa, gso, gea, geo, tri,
+    bc, pr, ro, rd, rl, sl, rr, cc, kk, fr, rrf, cea, ceo, mext, fold, gsa, gso, gea, geo, tri,
     ka, ko, fs, dr_s, dr_r, dc_s, dc_r, dk_r, fd, drf, ced, gd, sst_s, sst_r,
     sem, lsem, ssem, rsem,
 ):
@@ -234,11 +235,9 @@
     ]
     for copy in copies:
         copy.start()
-    for i in range(EARLY):
-        weights(i).start()
     for copy in fields:
         copy.start()
-    for i in range(EARLY, CHUNKS):
+    for i in range(CHUNKS):
         weights(i).start()
 
     for copy in targets:
@@ -280,10 +279,6 @@
             terms[pl.ds(at, 16), :] = r[:16, :128]
             terms[pl.ds(at + 16, 16), :] = r[16:, 128:]
 
-    @pl.loop(0, EARLY)
-    def _(i):
-        remap_chunk(i)
-
     for copy in fields:
         copy.wait()
     lane_a = lax.broadcasted_iota(jnp.int32, (64, 128), 1) >> 1
@@ -382,7 +377,7 @@
     def _():
         own_fold.start()
 
-    @pl.loop(EARLY, CHUNKS)
+    @pl.loop(0, CHUNKS)
     def _(i):
         remap_chunk(i)
 
@@ -397,12 +392,20 @@
 
     for dl in (0, 2, 1):
         send_to(always, send.at[dl * 3 + 2 - 2 * side], pr.at[dl], 16 + dl, 16 + dl, lon, partner)
-    for dl in range(3):
-        send_to(has_outer, send.at[dl * 3 + 2 * side], ro.at[dl], 19 + dl, 19 + dl, lon_at(dl - 1), outer)
+    straight = pl.ds(DETOUR, 8 - DETOUR)
+    for n, dl in enumerate((0, 2)):
+        block = dl * 3 + 2 * side
+        send_to(has_outer, send.at[block, pl.ds(0, DETOUR)], rd.at[n], 48 + n, 48 + n, lon, outer)
+        send_to(has_outer, send.at[block, straight], ro.at[dl, straight], 19 + dl, 19 + dl, lon_at(dl - 1), outer)
+    send_to(has_outer, send.at[3 + 2 * side], ro.at[1], 20, 20, lon, outer)
 
     @pl.when(jnp.logical_not(has_outer))
     def _():
         ro[...] = jnp.zeros_like(ro)
+        rd[...] = jnp.zeros_like(rd)
+
+    for dl in (0, 2):
+        ro[dl, 0:DETOUR] = jnp.zeros((DETOUR,) + ro.shape[2:], BF)
 
     for b, cond in ((0, has_south), (1, has_north)):
 
@@ -537,11 +540,18 @@
         arrive(always, pr.at[dl], 16 + dl)
     for n, dl in enumerate((0, 2)):
 
-        @pl.loop(0, 8)
+        @pl.loop(DETOUR, 8)
         def _(f, n=n, dl=dl):
             sl[n, f] = (send[3 * dl + 1, f].astype(F32) + pr[dl, f].astype(F32)).astype(BF)
 
-        send_to(always, sl.at[n], rl.at[n], 22 + n, 22 + n, lon_at(dl - 1), lat)
+        send_to(always, sl.at[n, straight], rl.at[n, straight], 22 + n, 22 + n, lon_at(dl - 1), lat)
+    for n, dl in enumerate((0, 2)):
+        arrive(has_outer, rd.at[n], 48 + n)
+        for f in range(DETOUR):
+            total = send[3 * dl + 1, f].astype(F32) + pr[dl, f].astype(F32) + rd[n, f].astype(F32)
+            sl[n, f] = total.astype(BF)
+        bent = pl.ds(0, DETOUR)
+        send_to(always, sl.at[n, bent], rl.at[n, bent], 50 + n, 50 + n, lon_at(dl - 1), lat)
 
     @pl.loop(0, 8)
     def _(i):
@@ -591,14 +601,26 @@
         for j, y in enumerate(parts):
             stepped[v, first + j] = y
 
+    def atm_mix(n):
+        v = n // 4
+        at = pl.multiple_of(lax.rem(n, 4) * 16, 16)
+        mixed = dot3(ka[0], ka[1], stepped[v, :, pl.ds(at, 16), :].reshape(256, 256))
+        stepped[v, :, pl.ds(at, 16), :] = mixed.reshape(16, 16, 256)
+
     @pl.loop(0, FIRST)
     def _(i):
         atm_group(i)
 
-    for dl in range(3):
-        arrive(has_outer, ro.at[dl], 19 + dl)
+    @pl.loop(0, MIXED, unroll=4)
+    def _(n):
+        atm_mix(n)
+
+    for dl in (0, 2):
+        arrive(has_outer, ro.at[dl, straight], 19 + dl)
+    arrive(has_outer, ro.at[1], 20)
     for n in range(2):
-        arrive(always, rl.at[n], 22 + n)
+        arrive(always, rl.at[n, straight], 22 + n)
+        arrive(always, rl.at[n, pl.ds(0, DETOUR)], 50 + n)
 
     @pl.loop(0, 8)
     def _(f):
@@ -696,12 +718,9 @@
                 back = 40 + direction[(-dl, -dn)]
                 slot = (1 - dl) * 3 + 1 - dn
                 send_to(lat_ok(dn), sst_s, sst_r.at[slot], n, back, lon_at(dl), lat + dn)
-    @pl.loop(0, 16, unroll=4)
+    @pl.loop(MIXED, 16, unroll=4)
     def _(n):
-        v = n // 4
-        at = pl.multiple_of(lax.rem(n, 4) * 16, 16)
-        mixed = dot3(ka[0], ka[1], stepped[v, :, pl.ds(at, 16), :].reshape(256, 256))
-        stepped[v, :, pl.ds(at, 16), :] = mixed.reshape(16, 16, 256)
+        atm_mix(n)
 
     sst_r[4] = sst_s[...]
     for dl, dn in around:
@@ -747,6 +766,7 @@
             pltpu.VMEM((4, 32, 48, 256), F32),
             pltpu.VMEM((3, 8, 96, 128), BF),
             pltpu.VMEM((3, 8, 96, 128), BF),
+            pltpu.VMEM((2, DETOUR, 96, 128), BF),
             pltpu.VMEM((2, 8, 96, 128), BF),
             pltpu.VMEM((2, 8, 96, 128), BF),
             pltpu.VMEM((2, 2, 144, 256), BF),
@@ -779,8 +799,8 @@
             pltpu.VMEM((9, 96, 128), BF),
             pltpu.SemaphoreType.DMA((8 + CHUNKS,)),
             pltpu.SemaphoreType.DMA((1,)),
-            pltpu.SemaphoreType.DMA((48,)),
-            pltpu.SemaphoreType.DMA((48,)),
+            pltpu.SemaphoreType.DMA((52,)),
+            pltpu.SemaphoreType.DMA((52,)),
         ],
         compiler_params=pltpu.CompilerParams(collective_id=0, has_side_effects=True, vmem_limit_bytes=36 * MIB),
         name="exchange",
@@ -805,7 +825,7 @@
     even = (row & 1) == 0
     ocean_out = lambda g: pltpu.make_async_copy(sea.at[pl.ds(g * 8, 8)], oce.at[pl.ds(g * 8, 8)], sem.at[6 + g])
 
-    @pl.loop(0, 8)
+    @pl.loop(0, 8, unroll=2)
     def _(g):
         v = g // 2
         for j in range(8):

time: 55.1 us -> 51.3 us (0.931); the launches traced: 54.3 us -> 51.1 us
  Pallas kernels: 53.6 us -> 50.4 us
    pallas_call x1, Pallas kernels: 48.1 us -> 45.2 us  [exchange(): pl.pallas_call(exchange_kernel, in_specs=[AWAY] * 8 + [HERE] * 3, out_spe...]
where the time goes in v3:
time: 51.3 us; the launch traced here: 51.1 us
  Pallas kernels  50.4 us (98%)
  between operations  0.67 us (1%)
    pallas_call x1, Pallas kernels, exchange(): pl.pallas_call(exchange_kernel, in_specs=[AWAY] * 8 + [HERE] * 3, out_spe...  45.2 us
    pallas_call x1, Pallas kernels, remap_back(): pl.pallas_call(back_kernel, in_specs=[HERE] * 9, out_specs=[AWAY] * 4, ou...  5.17 us

profile of v3, /device:TPU:97, one launch (start us, length us, event | category | flops | bytes accessed | tf_op | source)
XLA Modules:
  0.0 51.1 jit_solution(13671522062761274591)
XLA Ops:
  0.6 0.0 copy-start
  0.6 0.0 copy-start.1
  0.7 45.2 %exchange.1 = (bf16[128,3,128,128]{3,2,1,0:T(8,128)(2,1)S(1)}, f32[4,16,64,256]{3,2,1,0:T(8,128)S(1)}, f32[4,16,48,256]{3,2,1,0:T(8,128)S(1)}, f32[4,48,256]{2,1...) custom-call(f32[4,16,64,256]{3,2,1,0:T(8,128)} %atm_far.1, ...), custom_call_target="tpu_custom_call" | custom-call | tf_op jit(solution)/shard_map/exchange/pallas_call | solution.py:735
  45.9 0.0 copy-done
  45.9 0.0 copy-done.1
  45.9 5.2 %remap_back.1 = (f32[4,16,64,256]{3,2,1,0:T(8,128)}, f32[64,256]{1,0:T(8,128)}, f32[64,48,256]{2,1,0:T(8,128)}, f32[8,48,256]{2,1,0:T(8,128)}) custom-call(bf16[9,96,128]{2,1,0:T(8,128)(2,1)S(1)} %get-tuple-element.15.sst, s32[3,128]{1,0:T(4,128)S(1)} %bitcast.5, s32[3,128]{1,0:T(4,128)S(1)} %bitcast.7, f32[4,48,256]{2,1,0:T(8,128)S(1)} %get-tuple-element.16.q, ...), custom_call_target="tpu_custom_call" | custom-call | tf_op jit(solution)/shard_map/remap_back/pallas_call | solution.py:880
Async XLA Ops:
  0.6 45.3 %copy-start = (s32[128,3]{0,1:T(4,128)S(1)}, s32[128,3]{0,1:T(4,128)}, u32[]{:S(2)}) copy-start(s32[128,3]{0,1:T(4,128)} %param.15) | copy-start | bytes 4612
  0.6 45.3 %copy-start.1 = (s32[128,3]{0,1:T(4,128)S(1)}, s32[128,3]{0,1:T(4,128)}, u32[]{:S(2)}) copy-start(s32[128,3]{0,1:T(4,128)} %param.16) | copy-start | bytes 4612

commit v4 on v3

--- a/solution.py
+++ b/solution.py
@@ -17,7 +17,7 @@
 N_LAT = 16
 CHUNKS = 8
 FIRST = 4
-MIXED = 8
+MIXED = 4
 DETOUR = 2
 MIB = 2**20
 
@@ -540,7 +540,7 @@
         arrive(always, pr.at[dl], 16 + dl)
     for n, dl in enumerate((0, 2)):
 
-        @pl.loop(DETOUR, 8)
+        @pl.loop(DETOUR, 8, unroll=3)
         def _(f, n=n, dl=dl):
             sl[n, f] = (send[3 * dl + 1, f].astype(F32) + pr[dl, f].astype(F32)).astype(BF)
 
@@ -576,7 +576,7 @@
                 around = near(x, inner[j], south[j : j + 1], north[j : j + 1], turned(1 + k, j))
                 bc[v, 16 * k + first + j] = step_from(x, around, 0.2)
 
-    @pl.loop(0, 24, unroll=3)
+    @pl.loop(0, 24, unroll=6)
     def _(n):
         v = n // 6
         at = pl.multiple_of(lax.rem(n, 6) * 8, 8)
@@ -622,7 +622,7 @@
         arrive(always, rl.at[n, straight], 22 + n)
         arrive(always, rl.at[n, pl.ds(0, DETOUR)], 50 + n)
 
-    @pl.loop(0, 8)
+    @pl.loop(0, 8, unroll=4)
     def _(f):
         parts = [send[4, f], pr[1, f], rl[0, f], rl[1, f], ro[0, f], ro[1, f], ro[2, f]]
         total = functools.reduce(lambda x, y: x + y, [p.astype(F32) for p in parts])

time: 51.3 us -> 49.6 us (0.967)
  Pallas kernels: 50.4 us -> 48.8 us
    pallas_call x1, Pallas kernels: 45.2 us -> 43.6 us  [exchange(): pl.pallas_call(exchange_kernel, in_specs=[AWAY] * 8 + [HERE] * 3, out_spe...]
where the time goes in v4:
time: 49.6 us; the launch traced here: 49.5 us
  Pallas kernels  48.8 us (98%)
  between operations  0.67 us (1%)
    pallas_call x1, Pallas kernels, exchange(): pl.pallas_call(exchange_kernel, in_specs=[AWAY] * 8 + [HERE] * 3, out_spe...  43.6 us
    pallas_call x1, Pallas kernels, remap_back(): pl.pallas_call(back_kernel, in_specs=[HERE] * 9, out_specs=[AWAY] * 4, ou...  5.17 us

profile of v4, /device:TPU:97, one launch (start us, length us, event | category | flops | bytes accessed | tf_op | source)
XLA Modules:
  0.0 49.5 jit_solution(11753309157691388451)
XLA Ops:
  0.6 0.0 copy-start
  0.6 0.0 copy-start.1
  0.7 43.6 %exchange.1 = (bf16[128,3,128,128]{3,2,1,0:T(8,128)(2,1)S(1)}, f32[4,16,64,256]{3,2,1,0:T(8,128)S(1)}, f32[4,16,48,256]{3,2,1,0:T(8,128)S(1)}, f32[4,48,256]{2,1...) custom-call(f32[4,16,64,256]{3,2,1,0:T(8,128)} %atm_far.1, ...), custom_call_target="tpu_custom_call" | custom-call | tf_op jit(solution)/shard_map/exchange/pallas_call | solution.py:735
  44.3 0.0 copy-done
  44.3 0.0 copy-done.1
  44.3 5.2 %remap_back.1 = (f32[4,16,64,256]{3,2,1,0:T(8,128)}, f32[64,256]{1,0:T(8,128)}, f32[64,48,256]{2,1,0:T(8,128)}, f32[8,48,256]{2,1,0:T(8,128)}) custom-call(bf16[9,96,128]{2,1,0:T(8,128)(2,1)S(1)} %get-tuple-element.15.sst, s32[3,128]{1,0:T(4,128)S(1)} %bitcast.5, s32[3,128]{1,0:T(4,128)S(1)} %bitcast.7, f32[4,48,256]{2,1,0:T(8,128)S(1)} %get-tuple-element.16.q, ...), custom_call_target="tpu_custom_call" | custom-call | tf_op jit(solution)/shard_map/remap_back/pallas_call | solution.py:880
Async XLA Ops:
  0.6 43.6 %copy-start = (s32[128,3]{0,1:T(4,128)S(1)}, s32[128,3]{0,1:T(4,128)}, u32[]{:S(2)}) copy-start(s32[128,3]{0,1:T(4,128)} %param.15) | copy-start | bytes 4612
  0.6 43.6 %copy-start.1 = (s32[128,3]{0,1:T(4,128)S(1)}, s32[128,3]{0,1:T(4,128)}, u32[]{:S(2)}) copy-start(s32[128,3]{0,1:T(4,128)} %param.16) | copy-start | bytes 4612

commit v5 on v4

--- a/solution.py
+++ b/solution.py
@@ -722,11 +722,13 @@
     def _(n):
         atm_mix(n)
 
+    for finish in pending[: -len(around)]:
+        finish()
     sst_r[4] = sst_s[...]
     for dl, dn in around:
         arrive(lat_ok(dn), sst_r.at[(1 + dl) * 3 + 1 + dn], 40 + direction[(dl, dn)])
     sst_out[...] = sst_r[...]
-    for finish in pending:
+    for finish in pending[-len(around) :]:
         finish()
 
 

time: 49.6 us -> 49.6 us (level)
  no operation moved by 1% of the time
where the time goes in v5:
time: 49.6 us; the launch traced here: 49.4 us
  Pallas kernels  48.7 us (98%)
  between operations  0.67 us (1%)
    pallas_call x1, Pallas kernels, exchange(): pl.pallas_call(exchange_kernel, in_specs=[AWAY] * 8 + [HERE] * 3, out_spe...  43.6 us
    pallas_call x1, Pallas kernels, remap_back(): pl.pallas_call(back_kernel, in_specs=[HERE] * 9, out_specs=[AWAY] * 4, ou...  5.17 us

profile of v5, /device:TPU:97, one launch (start us, length us, event | category | flops | bytes accessed | tf_op | source)
XLA Modules:
  0.0 49.4 jit_solution(17655201462697621161)
XLA Ops:
  0.6 0.0 copy-start
  0.6 0.0 copy-start.1
  0.7 43.6 %exchange.1 = (bf16[128,3,128,128]{3,2,1,0:T(8,128)(2,1)S(1)}, f32[4,16,64,256]{3,2,1,0:T(8,128)S(1)}, f32[4,16,48,256]{3,2,1,0:T(8,128)S(1)}, f32[4,48,256]{2,1...) custom-call(f32[4,16,64,256]{3,2,1,0:T(8,128)} %atm_far.1, ...), custom_call_target="tpu_custom_call" | custom-call | tf_op jit(solution)/shard_map/exchange/pallas_call | solution.py:737
  44.2 0.0 copy-done
  44.2 0.0 copy-done.1
  44.3 5.2 %remap_back.1 = (f32[4,16,64,256]{3,2,1,0:T(8,128)}, f32[64,256]{1,0:T(8,128)}, f32[64,48,256]{2,1,0:T(8,128)}, f32[8,48,256]{2,1,0:T(8,128)}) custom-call(bf16[9,96,128]{2,1,0:T(8,128)(2,1)S(1)} %get-tuple-element.15.sst, s32[3,128]{1,0:T(4,128)S(1)} %bitcast.5, s32[3,128]{1,0:T(4,128)S(1)} %bitcast.7, f32[4,48,256]{2,1,0:T(8,128)S(1)} %get-tuple-element.16.q, ...), custom_call_target="tpu_custom_call" | custom-call | tf_op jit(solution)/shard_map/remap_back/pallas_call | solution.py:882
Async XLA Ops:
  0.6 43.6 %copy-start = (s32[128,3]{0,1:T(4,128)S(1)}, s32[128,3]{0,1:T(4,128)}, u32[]{:S(2)}) copy-start(s32[128,3]{0,1:T(4,128)} %param.15) | copy-start | bytes 4612
  0.6 43.6 %copy-start.1 = (s32[128,3]{0,1:T(4,128)S(1)}, s32[128,3]{0,1:T(4,128)}, u32[]{:S(2)}) copy-start(s32[128,3]{0,1:T(4,128)} %param.16) | copy-start | bytes 4612
